TPU v7x, 32 devices: a whole 2x2x4 slice. The times are simulated.
32 devices in a mesh: dp: 16 (over z, y, core), tensor: 2 (over x).
Axes of the slice: x: 2, y: 2, z: 4, core: 2. Of those that a mesh axis runs over, the one named last changes fastest.
Arguments:
- query_states: bfloat16 [3072, 4096], P('dp', 'tensor'), may hold values from -40 to 40
- doc_states: bfloat16 [3072, 4096], P('dp', 'tensor'), may hold values from -40 to 40
- proj_weight: bfloat16 [4096, 4096], P(None, 'tensor'), may hold values from -0.09375 to 0.09375
- left_proj: bfloat16 [4096, 64], replicated, may hold values from -0.09375 to 0.09375
- right_proj: bfloat16 [4096, 64], replicated, may hold values from -5 to 5
- positives: int32 [3072], P('dp'), may hold values from 0 to 3071
Outputs:
- query_features: float32 [3072, 4096], P('dp', 'tensor')
- doc_features: float32 [3072, 4096], P('dp', 'tensor')
All inputs are finite; a program needn't handle non-finite values.
Results may differ from a plain program's by a relative error of at most 0.0033.
Values may be sent and summed in bfloat16 or wider, within the bound.
A program may use at most 128 MiB of HBM per device.

v0:
```python
import jax
import jax.numpy as jnp
from jax import lax
from jax.sharding import PartitionSpec as P

epsilon = 1e-06
inverse_temp = 100.0


def outer_rows(left_side, right_side):
    return (left_side[:, :, None] * right_side[:, None, :]).reshape(left_side.shape[0], -1)


def local(query_states, doc_states, proj_weight, left_proj, right_proj, positives):
    tensor_count = lax.axis_size("tensor")
    tensor_rank = lax.axis_index("tensor")
    dp_count = lax.axis_size("dp")
    row_count = query_states.shape[0]
    doc_share = row_count // tensor_count
    left_share = left_proj.shape[1] // tensor_count
    query_full, doc_full = (
        lax.all_gather(query_states, "tensor", axis=1, tiled=True),
        lax.all_gather(doc_states, "tensor", axis=1, tiled=True),
    )
    query_raw = jnp.dot(query_full, proj_weight, preferred_element_type=jnp.float32)
    doc_raw = jnp.dot(doc_full, proj_weight, preferred_element_type=jnp.float32)
    query_sq, doc_sq = lax.psum(
        (jnp.sum(query_raw * query_raw, axis=1), jnp.sum(doc_raw * doc_raw, axis=1)), "tensor"
    )
    query_scale = lax.rsqrt(query_sq + epsilon)
    doc_scale = lax.rsqrt(doc_sq + epsilon)
    query_local = (query_raw * query_scale[:, None]).astype(jnp.bfloat16)
    doc_local = (doc_raw * doc_scale[:, None]).astype(jnp.bfloat16)
    query_unit, doc_unit = (
        lax.all_gather(query_local, "tensor", axis=1, tiled=True),
        lax.all_gather(doc_local, "tensor", axis=1, tiled=True),
    )
    doc_mine = lax.dynamic_slice_in_dim(doc_unit, tensor_rank * doc_share, doc_share, 0)
    doc_block = lax.all_gather(doc_mine, "dp", axis=0, tiled=True)
    scores = (
        lax.dot_general(
            query_unit, doc_block, (((1,), (1,)), ((), ())), preferred_element_type=jnp.float32
        )
        * inverse_temp
    )
    row_top = lax.pmax(jnp.max(scores, axis=1), "tensor")
    row_sum = lax.psum(jnp.sum(jnp.exp(scores - row_top[:, None]), axis=1), "tensor")
    lse = row_top + jnp.log(row_sum)
    column = jnp.arange(dp_count * doc_share, dtype=jnp.int32)
    doc_ids = column // doc_share * row_count + tensor_rank * doc_share + column % doc_share
    onehot = (positives[:, None] == doc_ids[None, :]).astype(jnp.float32)
    weights = (jnp.exp(scores - lse[:, None]) - onehot).astype(jnp.bfloat16)
    query_part = jnp.dot(weights, doc_block, preferred_element_type=jnp.float32) * inverse_temp
    left_query = jnp.dot(query_full, left_proj, preferred_element_type=jnp.float32)
    left_doc = jnp.dot(doc_full, left_proj, preferred_element_type=jnp.float32)
    left_query = lax.dynamic_slice_in_dim(left_query, tensor_rank * left_share, left_share, 1)
    left_doc = lax.dynamic_slice_in_dim(left_doc, tensor_rank * left_share, left_share, 1)
    right_wide = right_proj.astype(jnp.float32)
    inner_part = jnp.sum(query_unit.astype(jnp.float32) * query_part, axis=1)
    grad_proj = jnp.dot(query_part, right_wide, precision=lax.Precision.HIGHEST)
    inner_query, grad_query_proj = lax.psum((inner_part, grad_proj), "tensor")
    unit_query_proj = jnp.dot(query_unit, right_proj, preferred_element_type=jnp.float32)
    right_query = (grad_query_proj - inner_query[:, None] * unit_query_proj) * query_scale[:, None]
    doc_part = (
        lax.dot_general(
            weights, query_unit, (((0,), (0,)), ((), ())), preferred_element_type=jnp.float32
        )
        * inverse_temp
    )
    inner_doc_part = jnp.sum(doc_block.astype(jnp.float32) * doc_part, axis=1)
    doc_grad_proj = jnp.dot(doc_part, right_wide, precision=lax.Precision.HIGHEST)
    inner_doc, doc_grad_proj = (
        lax.psum_scatter(inner_doc_part, "dp", scatter_dimension=0, tiled=True),
        lax.psum_scatter(doc_grad_proj, "dp", scatter_dimension=0, tiled=True),
    )
    unit_doc_proj = jnp.dot(doc_mine, right_proj, preferred_element_type=jnp.float32)
    scale_mine = lax.dynamic_slice_in_dim(doc_scale, tensor_rank * doc_share, doc_share, 0)
    right_mine = (doc_grad_proj - inner_doc[:, None] * unit_doc_proj) * scale_mine[:, None]
    right_doc = lax.all_gather(right_mine, "tensor", axis=0, tiled=True)
    query_features = outer_rows(left_query, right_query)
    doc_features = outer_rows(left_doc, right_doc)
    return (query_features, doc_features)


def solution(mesh):
    placed = (P("dp", "tensor"), P("dp", "tensor"), P(None, "tensor"), P(), P(), P("dp"))
    return jax.shard_map(
        local,
        mesh=mesh,
        in_specs=placed,
        out_specs=(P("dp", "tensor"), P("dp", "tensor")),
        check_vma=False,
    )
```

profile of v0, /device:TPU:0, one launch (start us, length us, event | category | flops | bytes accessed | tf_op | source)
XLA Modules:
  0.0 368.5 jit_solution(1945472891729782824)
XLA Ops:
  7.2 0.0 all-gather.11.cloned.1.call-start
  7.2 0.7 all-gather.11.cloned.1.call-update
  7.9 0.0 all-gather.7.cloned.1.call-start
  8.0 0.7 all-gather.7.cloned.1.call-update
  8.7 0.0 all-gather.13.cloned.1.call-start
  8.7 30.8 %all-gather.11.cloned.1.call-done = bf16[192,4096]{1,0:T(8,128)(2,1)} async-done(((bf16[192,2048]{1,0:T(8,128)(2,1)}), bf16[192,4096]{1,0:T(8,128)(2,1)}) %all-gather.11.cloned.1.call-update) | async-done | bytes 1572880 | tf_op jit(solution)/shard_map/all_gather | solution.py:23
  39.5 10.8 %multiply_reduce_fusion.2 = (f32[192]{0:T(256)S(1)}, f32[192,2048]{1,0:T(8,128)}) fusion(bf16[192,4096]{1,0:T(8,128)(2,1)} %all-gather.11.cloned.1.call-done, bf16[4096,2048]{1,0:T(8,128)(2,1)} %param.8), kind=kOutput, calls=%fused_computation.8 | convolution fusion | flops 3222011648 | bytes 19923712 | tf_op jit(solution)/shard_map/dot_general | solution.py:26
  50.3 18.0 %all-gather.7.cloned.1.call-done = bf16[192,4096]{1,0:T(8,128)(2,1)} async-done(((bf16[192,2048]{1,0:T(8,128)(2,1)}), bf16[192,4096]{1,0:T(8,128)(2,1)}) %all-gather.7.cloned.1.call-update) | async-done | bytes 1572880 | tf_op jit(solution)/shard_map/all_gather | solution.py:22
  68.3 8.1 %multiply_reduce_fusion.3 = (f32[192]{0:T(256)S(1)}, f32[192,2048]{1,0:T(8,128)S(1)}) fusion(bf16[192,4096]{1,0:T(8,128)(2,1)} %all-gather.7.cloned.1.call-done, bf16[4096,2048]{1,0:T(8,128)(2,1)} %param.8), kind=kOutput, calls=%fused_computation.10 | convolution fusion | flops 3222011648 | bytes 19923712 | tf_op jit(solution)/shard_map/dot_general | solution.py:25
  76.4 4.9 %all-reduce.2 = (f32[192]{0:T(256)S(1)}, f32[192]{0:T(256)S(1)}) all-reduce(f32[192]{0:T(256)S(1)} %get-tuple-element.10, f32[192]{0:T(256)S(1)} %get-tuple-element.12), channel_id=1, replica_groups=mesh['dp'=16,'tensor'=2] {'tensor'}, use_global_device_ids=true, to_apply=%region_3.0 | all-reduce | flops 384 | bytes 3072 | tf_op jit(solution)/shard_map/psum | solution.py:27
  81.4 2.4 multiply_convert_fusion
  83.8 0.0 all-gather.13.cloned.1.call-update
  83.8 0.0 all-gather.9.cloned.1.call-start
  83.9 1.0 multiply_convert_fusion.1
  85.0 0.0 all-gather.15.cloned.1.call-start
  85.0 26.2 %all-gather.13.cloned.1.call-done = bf16[192,4096]{1,0:T(8,128)(2,1)} async-done(((bf16[192,2048]{1,0:T(8,128)(2,1)}), bf16[192,4096]{1,0:T(8,128)(2,1)}) %all-gather.13.cloned.1.call-update) | async-done | bytes 1572880 | tf_op jit(solution)/shard_map/all_gather | solution.py:36
  111.2 2.1 constant_dynamic-slice_fusion.1
  113.3 0.0 reduce-scatter.4.cloned.1.call-start
  113.4 0.6 dynamic-slice
  114.6 0.1 dynamic_slice.15
  114.7 0.6 fusion.23
  115.4 0.7 copy-done.5
  116.0 0.6 fusion.21
  116.7 23.7 %all-gather.9.cloned.1.call-done = bf16[192,4096]{1,0:T(8,128)(2,1)} async-done(((bf16[192,2048]{1,0:T(8,128)(2,1)}), bf16[192,4096]{1,0:T(8,128)(2,1)}) %all-gather.9.cloned.1.call-update) | async-done | bytes 1572880 | tf_op jit(solution)/shard_map/all_gather | solution.py:35
  140.4 102.9 %all-gather.15.cloned.1.call-done = bf16[1536,4096]{1,0:T(8,128)(2,1)} async-done(((bf16[96,4096]{1,0:T(8,128)(2,1)}), bf16[1536,4096]{1,0:T(8,128)(2,1)}) %all-gather.15.cloned.1.call-update) | async-done | bytes 12582928 | tf_op jit(solution)/shard_map/all_gather | solution.py:39
  243.4 7.9 %fusion.20 = (f32[192]{0:T(256)S(1)}, f32[192,1536]{1,0:T(8,128)S(1)}) fusion(bf16[192,4096]{1,0:T(8,128)(2,1)} %all-gather.9.cloned.1.call-done, bf16[1536,4096]{1,0:T(8,128)(2,1)} %all-gather.15.cloned.1.call-done), kind=kOutput, calls=%fused_computation.44 | convolution fusion | flops 2416508672 | bytes 15336192 | tf_op jit(solution)/shard_map/dot_general | solution.py:41
  251.2 4.9 %pmax.7 = f32[192]{0:T(256)S(1)} all-reduce(f32[192]{0:T(256)S(1)} %get-tuple-element.14), channel_id=1, replica_groups=mesh['dp'=16,'tensor'=2] {'tensor'}, use_global_device_ids=true, to_apply=%region_5.0 | all-reduce | flops 192 | bytes 1536 | tf_op jit(solution)/shard_map/pmax | solution.py:46
  256.2 0.3 exponential_reduce_fusion
  256.5 5.1 %psum.37 = f32[192]{0:T(256)S(1)} all-reduce(f32[192]{0:T(256)S(1)} %exponential_reduce_fusion), channel_id=1, replica_groups=mesh['dp'=16,'tensor'=2] {'tensor'}, use_global_device_ids=true, to_apply=%region_7.0 | all-reduce | flops 192 | bytes 1536 | tf_op jit(solution)/shard_map/psum | solution.py:47
  261.6 6.3 %multiply_reduce_fusion.1 = (f32[192]{0:T(256)S(1)}, f32[192,4096]{1,0:T(8,128)S(1)}) fusion(bf16[192,4096]{1,0:T(8,128)(2,1)S(1)} %copy-done.2, bf16[1536,4096]{1,0:T(8,128)(2,1)} %all-gather.15.cloned.1.call-done, f32[192,1536]{1,0:T(8,128)S(1)} %get-tuple-element.15, s32[1536]{0:T(1024)S(1)} %fusion.16, f32[192]{0:T(256)S(1)} %log_add_fusion, ...), kind=kOutput, calls=%fused_computation.5 | convolution fusion | flops 2420539136 | bytes 18489600 | tf_op jit(solution)/shard_map/dot_general | solution.py:53
  267.9 1.8 fusion.22
  269.7 13.1 %multiply_reduce_fusion = (f32[1536]{0:T(1024)S(1)}, f32[1536,4096]{1,0:T(8,128)}) fusion(bf16[1536,4096]{1,0:T(8,128)(2,1)} %all-gather.15.cloned.1.call-done, bf16[192,4096]{1,0:T(8,128)(2,1)S(1)} %copy-done.2, f32[192,1536]{1,0:T(8,128)S(1)} %get-tuple-element.15, s32[1536]{0:T(1024)S(1)} %fusion.16, f32[192]{0:T(256)S(1)} %log_add_fusion, s32[192]{0:T(256)S(1)} %copy-done.6), kind=kOutput, calls=%fused_computation | convolution fusion | flops 2442557952 | bytes 40515072 | tf_op jit(solution)/shard_map/dot_general | solution.py:65
  282.9 15.9 %fusion = f32[1536,64]{1,0:T(8,128)} fusion(bf16[4096,64]{0,1:T(8,128)(2,1)S(1)} %copy-done, f32[1536,4096]{1,0:T(8,128)} %get-tuple-element.19), kind=kOutput, calls=%fused_computation.1 | convolution fusion | flops 4838129664 | bytes 26083328
  298.7 0.0 reduce-scatter.4.cloned.1.call-update
  298.8 8.9 %all-reduce.1 = (f32[192,64]{0,1:T(8,128)S(1)}, f32[192]{0:T(256)S(1)}) all-reduce(f32[192,64]{0,1:T(8,128)S(1)} %fusion.22, f32[192]{0:T(256)S(1)} %get-tuple-element.16), channel_id=1, replica_groups=mesh['dp'=16,'tensor'=2] {'tensor'}, use_global_device_ids=true, to_apply=%region_8.9 | all-reduce | flops 12480 | bytes 99840 | tf_op jit(solution)/shard_map/psum | solution.py:61
  307.6 0.6 fusion.4
  308.3 0.2 broadcast_multiply_fusion.1
  308.5 1.7 copy.15
  310.2 30.0 %all-reduce = f32[1536]{0:T(1024)S(1)} all-reduce(f32[1536]{0:T(1024)S(1)} %get-tuple-element.18), channel_id=3, replica_groups=mesh['dp'=16,'tensor'=2] {'dp'}, use_global_device_ids=true, to_apply=%region_13.14.clone | all-reduce | flops 1536 | bytes 12288
  340.2 0.1 dynamic-slice.1
  340.3 13.3 %reduce-scatter.4.cloned.1.call-done = f32[96,64]{1,0:T(8,128)} async-done(((f32[1536,64]{1,0:T(8,128)}), f32[96,64]{1,0:T(8,128)}) %reduce-scatter.4.cloned.1.call-update) | async-done | bytes 24592
  353.7 0.9 copy.18
  354.5 0.4 fusion.7
  354.9 4.6 %all-gather = f32[2,96,64]{1,2,0:T(8,128)S(1)} all-gather(f32[1,96,64]{1,2,0:T(8,128)S(1)} %fusion.7), channel_id=1, replica_groups=mesh['dp'=16,'tensor'=2] {'tensor'}, dimensions={0}, use_global_device_ids=true | all-gather | bytes 73728 | tf_op jit(solution)/shard_map/all_gather | solution.py:79
  359.5 0.1 copy.14
  359.6 0.1 reshape.45
  359.7 0.2 broadcast_multiply_fusion
  359.9 1.7 copy.16
  (23 shorter events, 0.1 us)
Async XLA Ops:
  7.2 260.7 %copy-start = (bf16[4096,64]{0,1:T(8,128)(2,1)S(1)}, bf16[4096,64]{0,1:T(8,128)(2,1)}, u32[]{:S(2)}) copy-start(bf16[4096,64]{0,1:T(8,128)(2,1)} %param.10) | copy-start | bytes 1572868
  7.2 32.3 %all-gather.11.cloned.1.call-start = ((), (), s32[]{:S(2)}) async-start(), calls=%async_computation.3 | async-start | bytes 2359296 | tf_op jit(solution)/shard_map/all_gather | solution.py:23
  7.9 60.4 %all-gather.7.cloned.1.call-start = ((), (), s32[]{:S(2)}) async-start(), calls=%async_computation.1 | async-start | bytes 2359296 | tf_op jit(solution)/shard_map/all_gather | solution.py:22
  8.7 102.5 %all-gather.13.cloned.1.call-start = ((), (), s32[]{:S(2)}) async-start(), calls=%async_computation.4 | async-start | bytes 2359296 | tf_op jit(solution)/shard_map/all_gather | solution.py:36
  83.8 56.6 %all-gather.9.cloned.1.call-start = ((), (), s32[]{:S(2)}) async-start(), calls=%async_computation.2 | async-start | bytes 2359296 | tf_op jit(solution)/shard_map/all_gather | solution.py:35
  84.9 28.4 %copy-start.7 = (u32[32]{0:T(128)S(1)}, u32[32]{0:T(128)}, u32[]{:S(2)}) copy-start(u32[32]{0:T(128)} %constant.44) | copy-start | bytes 388
  84.9 29.8 %copy-start.3 = (bf16[4096,64]{0,1:T(8,128)(2,1)S(1)}, bf16[4096,64]{0,1:T(8,128)(2,1)}, u32[]{:S(2)}) copy-start(bf16[4096,64]{0,1:T(8,128)(2,1)} %param.9) | copy-start | bytes 1572868
  84.9 29.8 %copy-start.4 = (bf16[192,4096]{1,0:T(8,128)(2,1)S(1)}, bf16[192,4096]{1,0:T(8,128)(2,1)}, u32[]{:S(2)}) copy-start(bf16[192,4096]{1,0:T(8,128)(2,1)} %all-gather.11.cloned.1.call-done) | copy-start | bytes 4718596
  85.0 158.4 %all-gather.15.cloned.1.call-start = ((), (), s32[]{:S(2)}) async-start(), calls=%async_computation.5 | async-start | bytes 13369344 | tf_op jit(solution)/shard_map/all_gather | solution.py:39
  113.3 240.3 %reduce-scatter.4.cloned.1.call-start = ((), (), s32[]{:S(2)}) async-start(), calls=%async_computation.6 | async-start | bytes 835584
  114.6 1.4 copy-start.5
  116.7 145.0 %copy-start.6 = (s32[192]{0:T(256)S(1)}, s32[192]{0:T(256)}, u32[]{:S(2)}) copy-start(s32[192]{0:T(256)} %param.11) | copy-start | bytes 2308
  140.4 121.2 %copy-start.2 = (bf16[192,4096]{1,0:T(8,128)(2,1)S(1)}, bf16[192,4096]{1,0:T(8,128)(2,1)}, u32[]{:S(2)}) copy-start(bf16[192,4096]{1,0:T(8,128)(2,1)} %all-gather.9.cloned.1.call-done) | copy-start | bytes 4718596
  308.5 46.0 %copy-start.1 = (bf16[96,4096]{1,0:T(8,128)(2,1)S(1)}, bf16[96,4096]{1,0:T(8,128)(2,1)}, u32[]{:S(2)}) copy-start(bf16[96,4096]{1,0:T(8,128)(2,1)} %constant_dynamic-slice_fusion.1) | copy-start | bytes 2359300
Sparse Core Ops, SparseCore 0:
  9.6 29.8 all-gather.10
  41.0 27.1 all-gather.6
  84.0 27.2 all-gather.12
  113.2 27.1 all-gather.8
  142.6 100.7 all-gather.14
  298.9 54.7 reduce-scatter.3
where the time goes:
time: 369 us; the launch traced here: 368 us
  waiting for transfers between devices  216 us (59%)
  matrix products  66.2 us (18%)
  blocking collectives  58.5 us (16%)
  between operations  14.9 us (4%)
  local copies, waits for them, and re-layouts  7.94 us (2%)
  other arithmetic  4.28 us (1%)
    all_gather x1, waiting for transfers between devices, local(): doc_block = lax.all_gather(doc_mine, 'dp', axis=0, tiled=True)  103 us
    all_gather x1, waiting for transfers between devices, local(): lax.all_gather(doc_states, 'tensor', axis=1, tiled=True)  30.8 us
    unnamed x1, blocking collectives  30 us
    all_gather x1, waiting for transfers between devices, local(): lax.all_gather(doc_local, 'tensor', axis=1, tiled=True)  26.2 us
    all_gather x1, waiting for transfers between devices, local(): lax.all_gather(query_local, 'tensor', axis=1, tiled=True)  23.7 us
    all_gather x1, waiting for transfers between devices, local(): lax.all_gather(query_states, 'tensor', axis=1, tiled=True)  18 us
    unnamed x1, matrix products  15.9 us
    unnamed x7, waiting for transfers between devices  14.8 us
  transfers between devices with their start and end apart: 6, of which 6 were waited for; matrix products, arithmetic and copies ran while one was open for 5% of the time, Pallas kernels for 0%

commit v1 on v0

v1 whole, which is shorter than its diff:
```python
import jax
import jax.numpy as jnp
from jax import lax
from jax.sharding import PartitionSpec as P

epsilon = 1e-06
inverse_temp = 100.0
f32 = jnp.float32
bf16 = jnp.bfloat16


def outer_rows(left_side, right_side):
    return (left_side[:, :, None] * right_side[:, None, :]).reshape(left_side.shape[0], -1)


def split_hi_lo(value, axis):
    hi = value.astype(bf16)
    lo = (value - hi.astype(f32)).astype(bf16)
    return jnp.concatenate([hi, lo], axis=axis)


def halves(product, axis):
    size = product.shape[axis] // 2
    return lax.slice_in_dim(product, 0, size, axis=axis) + lax.slice_in_dim(product, size, 2 * size, axis=axis)


def gather_columns(block, count, rank):
    if count != 2:
        return lax.all_gather(block, "tensor", axis=1, tiled=True)
    other = lax.ppermute(block, "tensor", [(0, 1), (1, 0)])
    first = jnp.where(rank == 0, block, other)
    second = jnp.where(rank == 0, other, block)
    return jnp.concatenate([first, second], axis=1)


def projected(query_states, doc_states, proj_weight, left_proj):
    count = lax.axis_size("tensor")
    rank = lax.axis_index("tensor")
    rows = query_states.shape[0]
    left_share = left_proj.shape[1] // count
    full = gather_columns(jnp.concatenate([query_states, doc_states], axis=0), count, rank)
    raw = jnp.dot(full, proj_weight, preferred_element_type=f32)
    left_mine = lax.dynamic_slice_in_dim(left_proj, rank * left_share, left_share, 1)
    left = jnp.dot(full, left_mine, preferred_element_type=f32)
    scale = lax.rsqrt(lax.psum(jnp.sum(raw * raw, axis=1), "tensor") + epsilon)
    unit = (raw * scale[:, None]).astype(bf16)
    return unit, scale, left


def local(query_states, doc_states, proj_weight, left_proj, right_proj, positives):
    count = lax.axis_size("tensor")
    rank = lax.axis_index("tensor")
    dp_count = lax.axis_size("dp")
    rows = query_states.shape[0]
    share = rows // count
    unit, scale, left = projected(query_states, doc_states, proj_weight, left_proj)
    doc_local = unit[rows:]
    if count == 2:
        mine = lax.dynamic_slice_in_dim(doc_local, rank * share, share, 0)
        theirs = lax.dynamic_slice_in_dim(doc_local, (1 - rank) * share, share, 0)
        came = lax.ppermute(theirs, "tensor", [(0, 1), (1, 0)])
        first = jnp.where(rank == 0, mine, came)
        second = jnp.where(rank == 0, came, mine)
        doc_mine = jnp.concatenate([first, second], axis=1)
    else:
        doc_mine = lax.all_to_all(doc_local, "tensor", split_axis=0, concat_axis=1, tiled=True)
    doc_block = lax.all_gather(doc_mine, "dp", axis=0, tiled=True)
    query_unit = gather_columns(unit[:rows], count, rank)
    top = jnp.concatenate([query_unit, right_proj.T], axis=0)
    product = lax.dot_general(top, doc_block, (((1,), (1,)), ((), ())), preferred_element_type=f32)
    scores = product[:rows] * inverse_temp
    doc_right = product[rows:] * inverse_temp
    query_right = jnp.dot(query_unit, right_proj, preferred_element_type=f32)
    top_part = jnp.max(scores, axis=1)
    sum_part = jnp.sum(jnp.exp(scores - top_part[:, None]), axis=1)
    parts = lax.all_gather(jnp.stack([top_part, sum_part]), "tensor")
    row_top = jnp.max(parts[:, 0], axis=0)
    lse = row_top + jnp.log(jnp.sum(parts[:, 1] * jnp.exp(parts[:, 0] - row_top), axis=0))
    column = jnp.arange(dp_count * share, dtype=jnp.int32)
    doc_ids = column // share * rows + rank * share + column % share
    onehot = (positives[:, None] == doc_ids[None, :]).astype(f32)
    weights = (jnp.exp(scores - lse[:, None]) - onehot).astype(bf16)
    weighted = weights.astype(f32) * scores
    query_sum = halves(
        lax.dot_general(
            weights, split_hi_lo(doc_right, 0), (((1,), (1,)), ((), ())), preferred_element_type=f32
        ),
        1,
    )
    query_part = query_sum - jnp.sum(weighted, axis=1)[:, None] * query_right
    doc_sum = halves(
        lax.dot_general(
            split_hi_lo(query_right * inverse_temp, 1), weights, (((0,), (0,)), ((), ())),
            preferred_element_type=f32,
        ),
        0,
    )
    doc_part = doc_sum - jnp.sum(weighted, axis=0)[None, :] * (doc_right * (1.0 / inverse_temp))
    blocks = doc_part.reshape(doc_part.shape[0], dp_count, share).transpose(1, 2, 0)
    came = lax.all_to_all(blocks, "dp", split_axis=0, concat_axis=0, tiled=True)
    right_mine = jnp.sum(came, axis=0)
    right_doc = lax.all_gather(right_mine, "tensor", axis=0, tiled=True) * scale[rows:, None]
    right_query = lax.psum(query_part, "tensor") * scale[:rows, None]
    return (outer_rows(left[:rows], right_query), outer_rows(left[rows:], right_doc))


def solution(mesh):
    placed = (P("dp", "tensor"), P("dp", "tensor"), P(None, "tensor"), P(), P(), P("dp"))
    return jax.shard_map(
        local,
        mesh=mesh,
        in_specs=placed,
        out_specs=(P("dp", "tensor"), P("dp", "tensor")),
        check_vma=False,
    )
```

time: 369 us -> 247 us (0.67)
  waiting for transfers between devices: 216 us -> 160 us
  matrix products: 66.2 us -> 23 us
  blocking collectives: 58.5 us -> 22.7 us
  starting transfers between devices: 0.24 us -> 9.92 us
  other arithmetic: 4.28 us -> 9.23 us
    all_gather x4 -> x0, waiting for transfers between devices: 98.7 us -> none  [the longest x1 30.8 us: local(): lax.all_gather(doc_states, 'tensor', axis=1, tiled=True)]
    ppermute x0 -> x3, waiting for transfers between devices: none -> 57.2 us  [the longest x2 50.4 us: gather_columns(): other = lax.ppermute(block, 'tensor', [(0, 1), (1, 0)])]
    unnamed x1 -> x0, blocking collectives: 30 us -> none
    dot_general x10 -> x6, matrix products: 50.3 us -> 23 us  [the longest x1 12.7 us: projected(): raw = jnp.dot(full, proj_weight, preferred_element_type=f32)]
    unnamed x1 -> x0, matrix products: 15.9 us -> none
    unnamed x7 -> x1, waiting for transfers between devices: 14.8 us -> 0.02 us
    ppermute x0 -> x3, starting transfers between devices: none -> 6.31 us  [the longest x2 4.82 us: gather_columns(): other = lax.ppermute(block, 'tensor', [(0, 1), (1, 0)])]
    all_gather x1, waiting for transfers between devices: 103 us -> 97.7 us  [local(): doc_block = lax.all_gather(doc_mine, 'dp', axis=0, tiled=True)]
  transfers between devices with their start and end apart: 6 -> 5, of which waited for: 6 -> 5; matrix products, arithmetic and copies ran while one was open for 5% -> 2% of each run, Pallas kernels for 0% -> 0%
where the time goes in v1:
time: 247 us; the launch traced here: 246 us
  waiting for transfers between devices  160 us (65%)
  matrix products  23 us (9%)
  blocking collectives  22.7 us (9%)
  between operations  14.3 us (6%)
  starting transfers between devices  9.92 us (4%)
  other arithmetic  9.23 us (4%)
  local copies, waits for them, and re-layouts  7.09 us (3%)
    all_gather x1, waiting for transfers between devices, local(): doc_block = lax.all_gather(doc_mine, 'dp', axis=0, tiled=True)  97.7 us
    ppermute x2, waiting for transfers between devices, gather_columns(): other = lax.ppermute(block, 'tensor', [(0, 1), (1, 0)])  50.4 us
    dot_general x1, matrix products, projected(): raw = jnp.dot(full, proj_weight, preferred_element_type=f32)  12.7 us
    psum x1, blocking collectives, local(): right_query = lax.psum(query_part, 'tensor') * scale[:rows, None]  8.81 us
    ppermute x1, waiting for transfers between devices, local(): came = lax.ppermute(theirs, 'tensor', [(0, 1), (1, 0)])  6.8 us
    dot_general x1, matrix products, local(): lax.dot_general(top, doc_block, (((1,), (1,)), ((), ())), preferred_eleme...  6.48 us
    unnamed x24, local copies, waits for them, and re-layouts  5.61 us
    all_to_all x1, waiting for transfers between devices, local(): came = lax.all_to_all(blocks, 'dp', split_axis=0, concat_axis=0, tiled=True)  5.18 us
  transfers between devices with their start and end apart: 5, of which 5 were waited for; matrix products, arithmetic and copies ran while one was open for 2% of the time, Pallas kernels for 0%

profile of v1, /device:TPU:0, one launch (start us, length us, event | category | flops | bytes accessed | tf_op | source)
XLA Modules:
  0.0 246.3 jit_solution(6451464043087464326)
XLA Ops:
  7.2 0.0 copy-start
  7.2 0.0 all-gather.5.cloned.1.call-start
  7.2 1.3 constant_dynamic-update-slice_fusion.1
  8.5 0.1 copy-done.7
  8.6 0.1 constant_dynamic-update-slice_fusion
  8.7 3.0 %collective-permute-start = (bf16[384,2048]{1,0:T(8,128)(2,1)S(1)}, bf16[384,2048]{1,0:T(8,128)(2,1)}, u32[]{:S(2)}, u32[]{:S(2)}) collective-permute-start(bf16[384,2048]{1,0:T(8,128)(2,1)S(1)} %constant_dynamic-update-slice_fusion), channel_id=1, source_target_pairs={{0,1},{1,0},{2,3},{3,2},{4,5},{5,4},{6,7},{7,6},{8,9},{9,8},{10,11... | collective-permute-start | bytes 4718600 | tf_op jit(solution)/shard_map/ppermute | solution.py:30
  11.7 34.5 %collective-permute-done = bf16[384,2048]{1,0:T(8,128)(2,1)} collective-permute-done((bf16[384,2048]{1,0:T(8,128)(2,1)S(1)}, bf16[384,2048]{1,0:T(8,128)(2,1)}, u32[]{:S(2)}, u32[]{:S(2)}) %collective-permute-start) | collective-permute-done | bytes 1572896 | tf_op jit(solution)/shard_map/ppermute | solution.py:30
  46.2 1.6 broadcast_select_fusion.1
  47.8 0.0 copy-start.1
  47.8 0.0 copy-start.3
  47.8 12.7 %multiply_reduce_fusion = (f32[384]{0:T(512)S(1)}, f32[384,2048]{1,0:T(8,128)}) fusion(bf16[4096,2048]{1,0:T(8,128)(2,1)} %param.8, bf16[384,2048]{1,0:T(8,128)(2,1)S(1)} %get-tuple-element.16, bf16[384,2048]{1,0:T(8,128)(2,1)S(1)} %get-tuple-element.15), kind=kOutput, calls=%fused_computation.2 | convolution fusion | flops 6450314752 | bytes 23070208 | tf_op jit(solution)/shard_map/dot_general | solution.py:42
  60.6 4.9 %psum.14 = f32[384]{0:T(512)S(1)} all-reduce(f32[384]{0:T(512)S(1)} %get-tuple-element.32), channel_id=1, replica_groups=mesh['dp'=16,'tensor'=2] {'tensor'}, use_global_device_ids=true, to_apply=%region_1.2 | all-reduce | flops 384 | bytes 3072 | tf_op jit(solution)/shard_map/psum | solution.py:45
  65.5 2.1 multiply_convert_fusion
  67.6 0.1 slice.58
  67.7 1.8 collective-permute-start.1
  69.5 15.9 %collective-permute-done.1 = bf16[192,2048]{1,0:T(8,128)(2,1)} collective-permute-done((bf16[192,2048]{1,0:T(8,128)(2,1)S(1)}, bf16[192,2048]{1,0:T(8,128)(2,1)}, u32[]{:S(2)}, u32[]{:S(2)}) %collective-permute-start.1) | collective-permute-done | bytes 786464 | tf_op jit(solution)/shard_map/ppermute | solution.py:30
  85.5 2.6 %broadcast_select_fusion.3 = (bf16[192,2048]{1,0:T(8,128)(2,1)}, bf16[192,2048]{1,0:T(8,128)(2,1)}, bf16[192,2048]{1,0:T(8,128)(2,1)S(1)}) fusion(bf16[192,2048]{1,0:T(8,128)(2,1)} %collective-permute-done.1, pred[]{:T(512)S(6)} %eq.10, bf16[384,2048]{1,0:T(8,128)(2,1)S(1)} %multiply_convert_fusion), kind=kLoop, calls=%fused_computation.27 | loop fusion | flops 786432 | bytes 4718593 | tf_op jit(solution)/shard_map/jit(_where)/select_n | solution.py:31
  88.1 1.5 collective-permute-start.2
  89.6 6.8 %collective-permute-done.2 = bf16[96,2048]{1,0:T(8,128)(2,1)S(1)} collective-permute-done((bf16[96,2048]{1,0:T(8,128)(2,1)S(1)}, bf16[96,2048]{1,0:T(8,128)(2,1)S(1)}, u32[]{:S(2)}, u32[]{:S(2)}) %collective-permute-start.2) | collective-permute-done | bytes 393248 | tf_op jit(solution)/shard_map/ppermute | solution.py:61
  96.4 0.2 broadcast_select_fusion.5
  96.5 0.9 pad_maximum_fusion.3
  97.5 0.0 all-gather.5.cloned.1.call-update
  97.5 0.7 copy-done.2
  98.2 2.6 %fusion.7 = f32[384,32]{0,1:T(8,128)S(1)} fusion(bf16[384,2048]{1,0:T(8,128)(2,1)} %copy-done.3, bf16[384,2048]{1,0:T(8,128)(2,1)S(1)} %copy-done.2, bf16[4096,64]{0,1:T(8,128)(2,1)S(1)} %copy-done, s32[]{:T(128)S(6)} %select_n.68), kind=kOutput, calls=%fused_computation.10 | convolution fusion | flops 106954752 | bytes 3457028 | tf_op jit(solution)/shard_map/dot_general | solution.py:44
  100.8 0.1 fusion.48
  100.9 0.6 multiply_convert_fusion.1
  101.6 97.7 %all-gather.5.cloned.1.call-done = bf16[1536,4096]{1,0:T(8,128)(2,1)} async-done(((bf16[96,4096]{1,0:T(8,128)(2,1)}), bf16[1536,4096]{1,0:T(8,128)(2,1)}) %all-gather.5.cloned.1.call-update) | async-done | bytes 12582928 | tf_op jit(solution)/shard_map/all_gather | solution.py:67
  199.3 6.5 %fusion = f32[256,1536]{1,0:T(8,128)S(1)} fusion(bf16[1536,4096]{1,0:T(8,128)(2,1)} %all-gather.5.cloned.1.call-done, bf16[64,4096]{1,0:T(8,128)(2,1)S(1)} %bitcast.35, bf16[192,2048]{1,0:T(8,128)(2,1)S(1)} %copy-done.6, bf16[192,2048]{1,0:T(8,128)(2,1)S(1)} %copy-done.4), kind=kOutput, calls=%fused_computation.3 | convolution fusion | flops 3227516928 | bytes 16252928 | tf_op jit(solution)/shard_map/dot_general | solution.py:70
  205.8 0.2 fusion.14
  205.9 0.3 exponential_reduce_fusion
  206.3 4.3 %all-gather.1 = f32[2,2,192]{2,1,0:T(2,128)S(1)} all-gather(f32[1,2,192]{2,1,0:T(2,128)S(1)} %maximum_bitcast_fusion), channel_id=2, replica_groups=mesh['dp'=16,'tensor'=2] {'tensor'}, dimensions={0}, use_global_device_ids=true | all-gather | bytes 4608 | tf_op jit(solution)/shard_map/all_gather | solution.py:76
  210.7 0.6 fusion.12
  211.3 0.3 fusion.23
  211.6 0.1 subtract_convert_fusion.1
  211.7 0.2 reshape.53
  211.9 1.0 copy.47
  212.8 3.6 %all-to-all-start = ((f32[16,96,64]{1,2,0:T(8,128)}), f32[16,96,64]{1,2,0:T(8,128)S(1)}, u32[]{:S(2)}, u32[]{:S(2)}) async-start(f32[16,96,64]{1,2,0:T(8,128)} %bitcast.29), calls=%async_computation | async-start | bytes 1048576 | tf_op jit(solution)/shard_map/all_to_all | solution.py:100
  216.4 0.1 fusion.50
  216.5 0.3 fusion.16
  216.8 8.8 %psum.15 = f32[192,64]{0,1:T(8,128)S(1)} all-reduce(f32[192,64]{0,1:T(8,128)S(1)} %fusion.22), channel_id=1, replica_groups=mesh['dp'=16,'tensor'=2] {'tensor'}, use_global_device_ids=true, to_apply=%region_7.8 | all-reduce | flops 12288 | bytes 98304 | tf_op jit(solution)/shard_map/psum | solution.py:103
  225.6 5.2 %all-to-all-done = f32[16,96,64]{1,2,0:T(8,128)S(1)} async-done(((f32[16,96,64]{1,2,0:T(8,128)}), f32[16,96,64]{1,2,0:T(8,128)S(1)}, u32[]{:S(2)}, u32[]{:S(2)}) %all-to-all-start) | async-done | bytes 393248 | tf_op jit(solution)/shard_map/all_to_all | solution.py:100
  230.9 4.6 %all-gather.2 = f32[2,96,64]{1,2,0:T(8,128)S(1)} all-gather(f32[1,96,64]{1,2,0:T(8,128)S(1)} %bitcast.32), channel_id=1, replica_groups=mesh['dp'=16,'tensor'=2] {'tensor'}, dimensions={0}, use_global_device_ids=true | all-gather | bytes 73728 | tf_op jit(solution)/shard_map/all_gather | solution.py:102
  235.5 0.1 copy.34
  235.5 0.1 reshape.58
  235.6 0.2 broadcast_multiply_fusion
  235.9 1.7 copy.36
  237.6 0.2 broadcast_multiply_fusion.1
  237.8 1.7 copy.35
  (25 shorter events, 0.2 us)
Async XLA Ops:
  7.2 90.4 %copy-start = (bf16[4096,64]{0,1:T(8,128)(2,1)S(1)}, bf16[4096,64]{0,1:T(8,128)(2,1)}, u32[]{:S(2)}) copy-start(bf16[4096,64]{0,1:T(8,128)(2,1)} %param.9) | copy-start | bytes 1572868
  7.2 1.4 copy-start.7
  7.2 192.1 %all-gather.5.cloned.1.call-start = ((), (), s32[]{:S(2)}) async-start(), calls=%async_computation.1 | async-start | bytes 13369344 | tf_op jit(solution)/shard_map/all_gather | solution.py:67
  8.7 37.5 %collective-permute-start = (bf16[384,2048]{1,0:T(8,128)(2,1)S(1)}, bf16[384,2048]{1,0:T(8,128)(2,1)}, u32[]{:S(2)}, u32[]{:S(2)}) collective-permute-start(bf16[384,2048]{1,0:T(8,128)(2,1)S(1)} %constant_dynamic-update-slice_fusion), channel_id=1, source_target_pairs={{0,1},{1,0},{2,3},{3,2},{4,5},{5,4},{6,7},{7,6},{8,9},{9,8},{10,11... | collective-permute-start | bytes 4718600 | tf_op jit(solution)/shard_map/ppermute | solution.py:30
  47.8 12.8 %copy-start.1 = (bf16[384,2048]{1,0:T(8,128)(2,1)}, bf16[384,2048]{1,0:T(8,128)(2,1)S(1)}, u32[]{:S(2)}) copy-start(bf16[384,2048]{1,0:T(8,128)(2,1)S(1)} %get-tuple-element.15) | copy-start | bytes 4718596
  47.8 12.8 %copy-start.3 = (bf16[384,2048]{1,0:T(8,128)(2,1)}, bf16[384,2048]{1,0:T(8,128)(2,1)S(1)}, u32[]{:S(2)}) copy-start(bf16[384,2048]{1,0:T(8,128)(2,1)S(1)} %get-tuple-element.16) | copy-start | bytes 4718596
  67.7 17.7 %collective-permute-start.1 = (bf16[192,2048]{1,0:T(8,128)(2,1)S(1)}, bf16[192,2048]{1,0:T(8,128)(2,1)}, u32[]{:S(2)}, u32[]{:S(2)}) collective-permute-start(bf16[192,2048]{1,0:T(8,128)(2,1)S(1)} %slice.58), channel_id=1, source_target_pairs={{0,1},{1,0},{2,3},{3,2},{4,5},{5,4},{6,7},{7,6},{8,9},{9,8},{10,11... | collective-permute-start | bytes 2359304 | tf_op jit(solution)/shard_map/ppermute | solution.py:30
  88.1 8.3 %collective-permute-start.2 = (bf16[96,2048]{1,0:T(8,128)(2,1)S(1)}, bf16[96,2048]{1,0:T(8,128)(2,1)S(1)}, u32[]{:S(2)}, u32[]{:S(2)}) collective-permute-start(bf16[96,2048]{1,0:T(8,128)(2,1)S(1)} %constant_dynamic-slice_fusion), channel_id=1, source_target_pairs={{0,1},{1,0},{2,3},{3,2},{4,5},{5,4},{6,7},{7,6},{8,9},{9,8},{10,11... | collective-permute-start | bytes 1179656 | tf_op jit(solution)/shard_map/ppermute | solution.py:61
  96.5 1.7 copy-start.2
  98.2 2.7 %copy-start.4 = (bf16[192,2048]{1,0:T(8,128)(2,1)S(1)}, bf16[192,2048]{1,0:T(8,128)(2,1)}, u32[]{:S(2)}) copy-start(bf16[192,2048]{1,0:T(8,128)(2,1)} %get-tuple-element.17) | copy-start | bytes 2359300
  98.2 2.7 %copy-start.5 = (bf16[192,2048]{1,0:T(8,128)(2,1)S(1)}, bf16[192,2048]{1,0:T(8,128)(2,1)}, u32[]{:S(2)}) copy-start(bf16[192,2048]{1,0:T(8,128)(2,1)} %get-tuple-element.18) | copy-start | bytes 2359300
  98.2 2.7 %copy-start.9 = (bf16[4096,64]{0,1:T(8,128)(2,1)S(1)}, bf16[4096,64]{0,1:T(8,128)(2,1)}, u32[]{:S(2)}) copy-start(bf16[4096,64]{0,1:T(8,128)(2,1)} %param.10) | copy-start | bytes 1572868
  100.9 98.4 %copy-start.6 = (bf16[192,2048]{1,0:T(8,128)(2,1)S(1)}, bf16[192,2048]{1,0:T(8,128)(2,1)}, u32[]{:S(2)}) copy-start(bf16[192,2048]{1,0:T(8,128)(2,1)} %get-tuple-element.18) | copy-start | bytes 2359300
  205.8 4.9 %copy-start.8 = (s32[192]{0:T(256)S(1)}, s32[192]{0:T(256)}, u32[]{:S(2)}) copy-start(s32[192]{0:T(256)} %param.11) | copy-start | bytes 2308
  212.8 18.0 %all-to-all-start = ((f32[16,96,64]{1,2,0:T(8,128)}), f32[16,96,64]{1,2,0:T(8,128)S(1)}, u32[]{:S(2)}, u32[]{:S(2)}) async-start(f32[16,96,64]{1,2,0:T(8,128)} %bitcast.29), calls=%async_computation | async-start | bytes 1048576 | tf_op jit(solution)/shard_map/all_to_all | solution.py:100
Sparse Core Ops, SparseCore 0:
  97.6 101.6 all-gather.4

commit v2 on v1

--- a/solution.py
+++ b/solution.py
@@ -1,6 +1,10 @@
+import functools
+
 import jax
 import jax.numpy as jnp
 from jax import lax
+from jax.experimental import pallas as pl
+from jax.experimental.pallas import tpu as pltpu
 from jax.sharding import PartitionSpec as P
 
 epsilon = 1e-06
@@ -104,10 +108,288 @@
     return (outer_rows(left[:rows], right_query), outer_rows(left[rows:], right_doc))
 
 
+MESH = pl.DeviceIdType.MESH
+
+
+def dot_rows(a, b):
+    return lax.dot_general(a, b, (((1,), (1,)), ((), ())), preferred_element_type=f32)
+
+
+def dot_plain(a, b):
+    return lax.dot_general(a, b, (((1,), (0,)), ((), ())), preferred_element_type=f32)
+
+
+def hi_lo(value):
+    hi = value.astype(bf16)
+    return hi, (value - hi.astype(f32)).astype(bf16)
+
+
+def ring_kernel(
+    dp_count, rows, share, width,
+    top_ref, doc_ref, pos_ref, query_out, doc_out,
+    held, mine, out_buf, in_buf, stat_out, stat_in, qr_out, qr_in, qrt_out, qrt_in,
+    sum_out, sum_in, query_send, query_in, last_in,
+    right_send, left_send, ring_recv, half_recv, sib_send, sib_recv, x_send, x_recv,
+    all_send, all_recv, misc_send, misc_recv, local_sem,
+):
+    chips = dp_count // 2
+    half = chips // 2
+    me = lax.axis_index("dp")
+    side = lax.axis_index("tensor")
+    core = me % 2
+    chip = me // 2
+    spot = chip // 2 + (chip % 2) * (chips - 1 - 2 * (chip // 2))
+
+    def dp_at(step, flag):
+        q = (spot + step) % chips
+        upper = q // half
+        where = 2 * q + upper * (2 * (chips - 1 - q) + 1 - 2 * q)
+        return 2 * where + core + flag * (1 - 2 * core)
+
+    across = (me, 1 - side)
+    right = (dp_at(1, 0), side)
+    left = (dp_at(chips - 1, 0), side)
+    sibling = (dp_at(0, 1), side)
+
+    def send(src, dst, send_sem, recv_sem, device):
+        return pltpu.make_async_remote_copy(
+            src_ref=src, dst_ref=dst, send_sem=send_sem, recv_sem=recv_sem,
+            device_id=device, device_id_type=MESH,
+        )
+
+    barrier = pltpu.get_barrier_semaphore()
+    pl.semaphore_signal(barrier, inc=1, device_id=across, device_id_type=MESH)
+
+    @pl.loop(1, dp_count)
+    def _(b):
+        pl.semaphore_signal(
+            barrier, inc=1, device_id=(dp_at(b // 2, b % 2), side), device_id_type=MESH
+        )
+
+    pl.semaphore_wait(barrier, dp_count)
+
+    def slot(r):
+        return doc_ref if r % chips == 0 else held.at[2 * (r % chips)]
+
+    def to_right(s):
+        if s < half:
+            return send(slot(chips - s + 1), held.at[2 * (chips - s)], right_send.at[s],
+                        ring_recv.at[chips - s], right)
+        return send(slot(chips - s + 1).at[pl.ds(0, share)], held.at[2 * half, pl.ds(0, share)],
+                    right_send.at[s], ring_recv.at[half], right)
+
+    def to_left(s):
+        if s < half:
+            return send(slot(s - 1), held.at[2 * s], left_send.at[s], ring_recv.at[s], left)
+        return send(slot(s - 1).at[pl.ds(share, share)], held.at[2 * half, pl.ds(share, share)],
+                    left_send.at[s], half_recv, left)
+
+    def to_sibling(r):
+        return send(slot(r), held.at[2 * r + 1], sib_send.at[r], sib_recv.at[r], sibling)
+
+    def swap(b):
+        return send(out_buf.at[b], in_buf.at[b], x_send.at[b], x_recv.at[b], across)
+
+    def score(b):
+        top = top_ref[...]
+        out_buf[b] = dot_rows(top, held[b, pl.ds((1 - side) * share, share), :])
+        swap(b).start()
+        mine[b] = dot_rows(top, held[b, pl.ds(side * share, share), :])
+
+    to_right(1).start()
+    to_left(1).start()
+    to_sibling(0).start()
+    own = pltpu.make_async_copy(doc_ref, held.at[0], local_sem)
+    own.start()
+    qr_out[...] = dot_rows(top_ref[pl.ds(0, rows), :], top_ref[pl.ds(rows, width), :])
+    qrt_out[...] = dot_rows(top_ref[pl.ds(rows, width), :], top_ref[pl.ds(0, rows), :])
+    qr_swap = send(qr_out, qr_in, misc_send.at[0], misc_recv.at[0], across)
+    qrt_swap = send(qrt_out, qrt_in, misc_send.at[1], misc_recv.at[1], across)
+    qr_swap.start()
+    qrt_swap.start()
+    own.wait()
+    score(0)
+    to_sibling(0).wait_recv()
+    score(1)
+    for s in range(1, half):
+        to_right(s).wait_recv()
+        to_right(s + 1).start()
+        to_sibling(chips - s).start()
+        to_left(s).wait_recv()
+        to_left(s + 1).start()
+        to_sibling(s).start()
+        to_sibling(chips - s).wait_recv()
+        to_sibling(s).wait_recv()
+
+        @pl.loop(0, 4)
+        def _(k):
+            score(2 * (s + (k % 2) * (chips - 2 * s)) + k // 2)
+
+    to_right(half).wait_recv()
+    to_left(half).wait_recv()
+    to_sibling(half).start()
+    score(2 * half)
+    to_sibling(half).wait_recv()
+    score(2 * half + 1)
+    for s in range(1, half + 1):
+        to_right(s).wait_send()
+        to_left(s).wait_send()
+    for r in range(chips):
+        to_sibling(r).wait_send()
+
+    def add_up(b, top):
+        swap(b).wait()
+        total = mine[b] + in_buf[b]
+        mine[b] = total
+        return jnp.maximum(top, total[:rows] * inverse_temp)
+
+    top_wide = lax.fori_loop(0, dp_count, add_up, jnp.full((rows, share), -jnp.inf, f32))
+    top_mine = jnp.max(top_wide, axis=1, keepdims=True)
+
+    def add_exp(b, total):
+        return total + jnp.exp(mine[b, pl.ds(0, rows), :] * inverse_temp - top_mine)
+
+    sum_wide = lax.fori_loop(0, dp_count, add_exp, jnp.zeros((rows, share), f32))
+    sum_mine = jnp.sum(sum_wide, axis=1, keepdims=True)
+    diagonal = lax.broadcasted_iota(jnp.int32, (rows, rows), 0) == lax.broadcasted_iota(
+        jnp.int32, (rows, rows), 1
+    )
+
+    def as_row(col):
+        return jnp.sum(jnp.where(diagonal, col, 0.0), axis=0, keepdims=True)
+
+    def as_col(row):
+        return jnp.sum(jnp.where(diagonal, row, 0.0), axis=1, keepdims=True)
+
+    stat_out[...] = jnp.concatenate(
+        [jnp.broadcast_to(as_row(top_mine), (4, rows)), jnp.broadcast_to(as_row(sum_mine), (4, rows))],
+        axis=0,
+    )
+    stat_swap = send(stat_out, stat_in, misc_send.at[2], misc_recv.at[2], across)
+    stat_swap.start()
+    qr_swap.wait()
+    qrt_swap.wait()
+    query_right = qr_out[...] + qr_in[...]
+    turned_hi, turned_lo = hi_lo((qrt_out[...] + qrt_in[...]) * inverse_temp)
+    stat_swap.wait()
+    stats = stat_in[...]
+    top_other = as_col(stats[0:1])
+    sum_other = as_col(stats[4:5])
+    row_top = jnp.maximum(top_mine, top_other)
+    lse = row_top + jnp.log(
+        sum_mine * jnp.exp(top_mine - row_top) + sum_other * jnp.exp(top_other - row_top)
+    )
+    positives = pos_ref[...]
+
+    def share_out(b):
+        return send(
+            sum_out.at[b], sum_in.at[2 * ((chips - b // 2) % chips) + b % 2], all_send.at[b],
+            all_recv.at[2 * ((chips - b // 2) % chips) + b % 2], (dp_at(b // 2, b % 2), side),
+        )
+
+    def gradients(b, carry):
+        query_sum, inner_wide = carry
+        scores = mine[b, pl.ds(0, rows), :] * inverse_temp
+        doc_right = mine[b, pl.ds(rows, width), :]
+        ids = lax.broadcasted_iota(jnp.int32, (rows, share), 1) + (
+            dp_at(b // 2, b % 2) * rows + side * share
+        )
+        onehot = jnp.where(positives == ids, 1.0, 0.0)
+        weights = (jnp.exp(scores - lse) - onehot).astype(bf16)
+        weighted = weights.astype(f32) * scores
+        right_hi, right_lo = hi_lo(doc_right * inverse_temp)
+        query_sum = query_sum + dot_rows(weights, right_hi) + dot_rows(weights, right_lo)
+        sum_out[b] = (
+            dot_plain(turned_hi, weights) + dot_plain(turned_lo, weights)
+            - jnp.sum(weighted, axis=0, keepdims=True) * doc_right
+        )
+        return query_sum, inner_wide + weighted
+
+    carry = (jnp.zeros((rows, width), f32), jnp.zeros((rows, share), f32))
+
+    def step(b, carry):
+        carry = gradients(b, carry)
+        share_out(b).start()
+        return carry
+
+    carry = lax.fori_loop(1, dp_count, step, carry)
+    query_sum, inner_wide = gradients(0, carry)
+    query_send[...] = query_sum - jnp.sum(inner_wide, axis=1, keepdims=True) * query_right
+    query_swap = send(query_send, query_in, misc_send.at[3], misc_recv.at[3], across)
+    query_swap.start()
+
+    @pl.loop(1, dp_count)
+    def _(b):
+        share_out(b).wait()
+
+    def collect(b, total):
+        return total + sum_in[b]
+
+    doc_sum = lax.fori_loop(1, dp_count, collect, sum_out[0])
+    doc_out[side] = doc_sum
+    last_swap = send(doc_out.at[side], last_in, misc_send.at[4], misc_recv.at[4], across)
+    last_swap.start()
+    query_swap.wait()
+    query_out[...] = query_send[...] + query_in[...]
+    last_swap.wait()
+    doc_out[1 - side] = last_in[...]
+
+
+def ring_gradients(top, docs, positives, dp_count, rows, share, width):
+    chips = dp_count // 2
+    depth = docs.shape[1]
+    dma = pltpu.SemaphoreType.DMA
+    sums = pltpu.VMEM((dp_count, width, share), f32)
+    parts = pltpu.VMEM((dp_count, rows + width, share), f32)
+    vmem = pl.BlockSpec(memory_space=pltpu.VMEM)
+    return pl.pallas_call(
+        functools.partial(ring_kernel, dp_count, rows, share, width),
+        out_shape=(
+            jax.ShapeDtypeStruct((rows, width), f32),
+            jax.ShapeDtypeStruct((2, width, share), f32),
+        ),
+        in_specs=[vmem] * 3,
+        out_specs=(vmem, vmem),
+        scratch_shapes=[
+            pltpu.VMEM((dp_count, rows, depth), bf16),
+            parts, parts, parts,
+            pltpu.VMEM((8, rows), f32), pltpu.VMEM((8, rows), f32),
+            pltpu.VMEM((rows, width), f32), pltpu.VMEM((rows, width), f32),
+            pltpu.VMEM((width, rows), f32), pltpu.VMEM((width, rows), f32),
+            sums, sums,
+            pltpu.VMEM((rows, width), f32), pltpu.VMEM((rows, width), f32),
+            pltpu.VMEM((width, share), f32),
+            dma((chips,)), dma((chips,)), dma((chips,)), dma, dma((chips,)), dma((chips,)),
+            dma((dp_count,)), dma((dp_count,)), dma((dp_count,)), dma((dp_count,)),
+            dma((5,)), dma((5,)), dma,
+        ],
+        compiler_params=pltpu.CompilerParams(
+            collective_id=0, has_side_effects=True, vmem_limit_bytes=44 * 2**20
+        ),
+    )(top, docs, positives)
+
+
+def local_ring(query_states, doc_states, proj_weight, left_proj, right_proj, positives):
+    rank = lax.axis_index("tensor")
+    rows = query_states.shape[0]
+    share = rows // 2
+    depth = proj_weight.shape[1]
+    unit, scale, left = projected(query_states, doc_states, proj_weight, left_proj)
+    right_mine = lax.dynamic_slice_in_dim(right_proj, rank * depth, depth, 0)
+    top = jnp.concatenate([unit[:rows], right_mine.T], axis=0)
+    right_query, right_doc = ring_gradients(
+        top, unit[rows:], positives[:, None], lax.axis_size("dp"), rows, share, right_proj.shape[1]
+    )
+    right_query = right_query * scale[:rows, None]
+    right_doc = right_doc.transpose(0, 2, 1).reshape(rows, -1) * scale[rows:, None]
+    return (outer_rows(left[:rows], right_query), outer_rows(left[rows:], right_doc))
+
+
 def solution(mesh):
+    ring = mesh.shape["tensor"] == 2 and mesh.shape["dp"] % 4 == 0 and mesh.shape["dp"] >= 8
     placed = (P("dp", "tensor"), P("dp", "tensor"), P(None, "tensor"), P(), P(), P("dp"))
     return jax.shard_map(
-        local,
+        local_ring if ring else local,
         mesh=mesh,
         in_specs=placed,
         out_specs=(P("dp", "tensor"), P("dp", "tensor")),

time: 247 us -> 173 us (0.70)
  waiting for transfers between devices: 160 us -> 34.3 us
  Pallas kernels: 0 us -> 102 us
  blocking collectives: 22.7 us -> 4.92 us
  between operations: 14.3 us -> 0.79 us
  matrix products: 23 us -> 13.6 us
  starting transfers between devices: 9.92 us -> 3 us
  other arithmetic: 9.23 us -> 5.86 us
    pallas_call x0 -> x1, Pallas kernels: none -> 102 us  [ring_gradients(): pl.pallas_call(functools.partial(ring_kernel, dp_count, rows, share, widt...]
    all_gather x1 -> x0, waiting for transfers between devices: 97.7 us -> none  [local(): doc_block = lax.all_gather(doc_mine, 'dp', axis=0, tiled=True)]
    ppermute x2 -> x1, waiting for transfers between devices: 50.4 us -> 34.3 us  [gather_columns(): other = lax.ppermute(block, 'tensor', [(0, 1), (1, 0)])]
    all_gather x2 -> x0, blocking collectives: 8.93 us -> none  [the longest x1 4.59 us: local(): lax.all_gather(right_mine, 'tensor', axis=0, tiled=True)]
    psum x1 -> x0, blocking collectives: 8.81 us -> none  [local(): right_query = lax.psum(query_part, 'tensor') * scale[:rows, None]]
    dot_general x4 -> x0, matrix products: 7.7 us -> none  [the longest x1 6.48 us: local(): lax.dot_general(top, doc_block, (((1,), (1,)), ((), ())), preferred_eleme...]
    ppermute x1 -> x0, waiting for transfers between devices: 6.8 us -> none  [local(): came = lax.ppermute(theirs, 'tensor', [(0, 1), (1, 0)])]
    all_to_all x1 -> x0, waiting for transfers between devices: 5.18 us -> none  [local(): came = lax.all_to_all(blocks, 'dp', split_axis=0, concat_axis=0, tiled=True)]
  transfers between devices with their start and end apart: 5 -> 1, of which waited for: 5 -> 1; matrix products, arithmetic and copies ran while one was open for 2% -> 0% of each run, Pallas kernels for 0% -> 0%
where the time goes in v2:
time: 173 us
  Pallas kernels  102 us (59%)
  waiting for transfers between devices  34.3 us (20%)
  matrix products  13.6 us (8%)
  local copies, waits for them, and re-layouts  8.31 us (5%)
  other arithmetic  5.86 us (3%)
  blocking collectives  4.92 us (3%)
  starting transfers between devices  3 us (2%)
    pallas_call x1, Pallas kernels, ring_gradients(): pl.pallas_call(functools.partial(ring_kernel, dp_count, rows, share, widt...  102 us
    ppermute x1, waiting for transfers between devices, gather_columns(): other = lax.ppermute(block, 'tensor', [(0, 1), (1, 0)])  34.3 us
    dot_general x1, matrix products, projected(): raw = jnp.dot(full, proj_weight, preferred_element_type=f32)  12.6 us
    unnamed x19, local copies, waits for them, and re-layouts  7.56 us
    psum x1, blocking collectives, projected(): scale = lax.rsqrt(lax.psum(jnp.sum(raw * raw, axis=1), 'tensor') + epsilon)  4.92 us
  transfers between devices with their start and end apart: 1, of which 1 were waited for; matrix products, arithmetic and copies ran while one was open for 0% of the time, Pallas kernels for 0%

profile of v2, /device:TPU:0, one launch (start us, length us, event | category | flops | bytes accessed | tf_op | source)
XLA Modules:
  0.0 173.2 jit_solution(5683723278595355859)
XLA Ops:
  0.6 0.0 copy-start
  0.6 0.0 copy-start.5
  0.7 0.0 copy-start.6
  0.7 1.3 constant_dynamic-update-slice_fusion.1
  2.0 0.1 copy-done.5
  2.1 0.1 constant_dynamic-update-slice_fusion
  2.1 3.0 %collective-permute-start = (bf16[384,2048]{1,0:T(8,128)(2,1)S(1)}, bf16[384,2048]{1,0:T(8,128)(2,1)}, u32[]{:S(2)}, u32[]{:S(2)}) collective-permute-start(bf16[384,2048]{1,0:T(8,128)(2,1)S(1)} %constant_dynamic-update-slice_fusion), channel_id=1, source_target_pairs={{0,1},{1,0},{2,3},{3,2},{4,5},{5,4},{6,7},{7,6},{8,9},{9,8},{10,11... | collective-permute-start | bytes 4718600 | tf_op jit(solution)/shard_map/ppermute | solution.py:34
  5.1 0.0 copy-done.6
  5.1 0.1 copy.10.pos_ref
  5.3 0.0 copy-done
  5.3 34.3 %collective-permute-done = bf16[384,2048]{1,0:T(8,128)(2,1)} collective-permute-done((bf16[384,2048]{1,0:T(8,128)(2,1)S(1)}, bf16[384,2048]{1,0:T(8,128)(2,1)}, u32[]{:S(2)}, u32[]{:S(2)}) %collective-permute-start) | collective-permute-done | bytes 1572896 | tf_op jit(solution)/shard_map/ppermute | solution.py:34
  39.6 1.6 broadcast_select_fusion.1
  41.3 0.0 copy-start.1
  41.3 0.0 copy-start.3
  41.3 12.6 %multiply_reduce_fusion = (f32[384]{0:T(512)S(1)}, f32[384,2048]{1,0:T(8,128)}) fusion(bf16[4096,2048]{1,0:T(8,128)(2,1)} %param.8, bf16[384,2048]{1,0:T(8,128)(2,1)S(1)} %get-tuple-element.9, bf16[384,2048]{1,0:T(8,128)(2,1)S(1)} %get-tuple-element.8), kind=kOutput, calls=%fused_computation.2 | convolution fusion | flops 6450314752 | bytes 23070208 | tf_op jit(solution)/shard_map/dot_general | solution.py:46
  53.9 0.0 copy-done.1
  53.9 0.0 copy-done.3
  53.9 4.9 %psum.7 = f32[384]{0:T(512)S(1)} all-reduce(f32[384]{0:T(512)S(1)} %get-tuple-element.16), channel_id=1, replica_groups=mesh['dp'=16,'tensor'=2] {'tensor'}, use_global_device_ids=true, to_apply=%region_1.2 | all-reduce | flops 384 | bytes 3072 | tf_op jit(solution)/shard_map/psum | solution.py:49
  58.8 0.1 fusion.8
  58.9 0.0 copy-start.7
  58.9 2.2 %multiply_convert_fusion = bf16[384,2048]{1,0:T(8,128)(2,1)S(1)} fusion(f32[384,2048]{1,0:T(8,128)} %get-tuple-element.17, f32[384]{0:T(512)S(1)} %add_rsqrt_fusion), kind=kLoop, calls=%fused_computation.1 | loop fusion | flops 1572864 | bytes 4720128 | tf_op jit(solution)/shard_map/convert_element_type | solution.py:50
  61.1 0.0 copy-start.2
  61.1 0.0 copy-start.4
  61.1 0.2 fusion.6
  61.3 0.0 copy-done.7
  61.3 1.2 copy-done.2
  62.5 0.5 copy-done.4
  63.0 1.0 fusion.1
  64.0 0.1 fusion.7
  64.1 0.1 pad_maximum_fusion.3.top_ref
  64.2 102.4 %shard_map.77 = (f32[192,64]{1,0:T(8,128)S(1)}, f32[2,64,96]{2,1,0:T(8,128)S(1)}) custom-call(bf16[256,2048]{1,0:T(8,128)(2,1)S(1)} %pad_maximum_fusion.3.top_ref, bf16[192,2048]{1,0:T(8,128)(2,1)S(1)} %get-tuple-element.10.doc_ref, s32[192,1]{1,0:T(8,128)S(1)} %copy.10.pos_ref), custom_call_target="tpu_custom_call" | custom-call | tf_op jit(solution)/shard_map/pallas_call | solution.py:345
  166.6 0.1 broadcast_multiply_fusion.2
  166.7 0.1 copy.11
  166.7 0.1 copy.12
  166.8 0.1 reshape.36
  166.9 1.9 %broadcast_multiply_fusion = (f32[192,32,64]{0,2,1:T(8,128)}, f32[192,32,64]{0,2,1:T(8,128)S(1)}) fusion(f32[192,64]{0,1:T(8,128)S(1)} %broadcast_multiply_fusion.3, f32[192,32]{0,1:T(8,128)S(1)} %get-tuple-element.12, f32[192,64]{0,1:T(8,128)S(1)} %copy.11, f32[192,32]{0,1:T(8,128)S(1)} %get-tuple-element.13), kind=kLoop, calls=%fused_computation.8 | loop fusion | flops 786432 | bytes 3293184 | tf_op jit(solution)/shard_map/mul | solution.py:17
  168.8 2.8 %copy.14 = f32[192,2048]{1,0:T(8,128)} copy(f32[192,2048]{0,1:T(8,128)} %bitcast.11) | data formatting | bytes 3145728
  171.5 1.7 copy.13
  (3 shorter events, 0.0 us)
Async XLA Ops:
  0.6 4.6 %copy-start = (bf16[4096,64]{0,1:T(8,128)(2,1)S(1)}, bf16[4096,64]{0,1:T(8,128)(2,1)}, u32[]{:S(2)}) copy-start(bf16[4096,64]{0,1:T(8,128)(2,1)} %param.10) | copy-start | bytes 1572868
  0.6 1.4 copy-start.5
  0.7 4.5 %copy-start.6 = (s32[192]{0:T(256)S(1)}, s32[192]{0:T(256)}, u32[]{:S(2)}) copy-start(s32[192]{0:T(256)} %param.11) | copy-start | bytes 2308
  2.1 37.5 %collective-permute-start = (bf16[384,2048]{1,0:T(8,128)(2,1)S(1)}, bf16[384,2048]{1,0:T(8,128)(2,1)}, u32[]{:S(2)}, u32[]{:S(2)}) collective-permute-start(bf16[384,2048]{1,0:T(8,128)(2,1)S(1)} %constant_dynamic-update-slice_fusion), channel_id=1, source_target_pairs={{0,1},{1,0},{2,3},{3,2},{4,5},{5,4},{6,7},{7,6},{8,9},{9,8},{10,11... | collective-permute-start | bytes 4718600 | tf_op jit(solution)/shard_map/ppermute | solution.py:34
  41.3 12.6 %copy-start.1 = (bf16[384,2048]{1,0:T(8,128)(2,1)}, bf16[384,2048]{1,0:T(8,128)(2,1)S(1)}, u32[]{:S(2)}) copy-start(bf16[384,2048]{1,0:T(8,128)(2,1)S(1)} %get-tuple-element.8) | copy-start | bytes 4718596
  41.3 12.6 %copy-start.3 = (bf16[384,2048]{1,0:T(8,128)(2,1)}, bf16[384,2048]{1,0:T(8,128)(2,1)S(1)}, u32[]{:S(2)}) copy-start(bf16[384,2048]{1,0:T(8,128)(2,1)S(1)} %get-tuple-element.9) | copy-start | bytes 4718596
  58.9 2.4 %copy-start.7 = (bf16[4096,64]{0,1:T(8,128)(2,1)S(1)}, bf16[4096,64]{0,1:T(8,128)(2,1)}, u32[]{:S(2)}) copy-start(bf16[4096,64]{0,1:T(8,128)(2,1)} %param.9) | copy-start | bytes 1572868
  61.1 1.4 copy-start.2
  61.1 1.9 %copy-start.4 = (bf16[384,2048]{1,0:T(8,128)(2,1)S(1)}, bf16[384,2048]{1,0:T(8,128)(2,1)}, u32[]{:S(2)}) copy-start(bf16[384,2048]{1,0:T(8,128)(2,1)} %copy-done.3) | copy-start | bytes 4718596

commit v3 on v2

--- a/solution.py
+++ b/solution.py
@@ -124,14 +124,23 @@
     return hi, (value - hi.astype(f32)).astype(bf16)
 
 
+pieces = 4
+tiles = 4
+
+
 def ring_kernel(
     dp_count, rows, share, width,
-    top_ref, doc_ref, pos_ref, query_out, doc_out,
+    query_ref, doc_ref, weight_ref, left_ref, right_ref, pos_ref,
+    query_out, doc_out, scale_out, left_out,
+    weight, query_raw, doc_raw, query_came, doc_came, top_ref,
     held, mine, out_buf, in_buf, stat_out, stat_in, qr_out, qr_in, qrt_out, qrt_in,
     sum_out, sum_in, query_send, query_in, last_in,
     right_send, left_send, ring_recv, half_recv, sib_send, sib_recv, x_send, x_recv,
-    all_send, all_recv, misc_send, misc_recv, local_sem,
+    all_send, all_recv, misc_send, misc_recv, local_sem, state_send, state_recv,
 ):
+    depth = query_ref.shape[1]
+    piece = depth // pieces
+    tile = depth // tiles
     chips = dp_count // 2
     half = chips // 2
     me = lax.axis_index("dp")
@@ -157,6 +166,15 @@
             device_id=device, device_id_type=MESH,
         )
 
+    loads = [
+        pltpu.make_async_copy(
+            weight_ref.at[pl.ds(pl.multiple_of(which * depth, depth), depth)], weight.at[i], local_sem.at[i]
+        )
+        for i, which in enumerate((side, 1 - side))
+    ]
+    for load in loads:
+        load.start()
+
     barrier = pltpu.get_barrier_semaphore()
     pl.semaphore_signal(barrier, inc=1, device_id=across, device_id_type=MESH)
 
@@ -169,7 +187,7 @@
     pl.semaphore_wait(barrier, dp_count)
 
     def slot(r):
-        return doc_ref if r % chips == 0 else held.at[2 * (r % chips)]
+        return held.at[2 * (r % chips)]
 
     def to_right(s):
         if s < half:
@@ -196,21 +214,100 @@
         swap(b).start()
         mine[b] = dot_rows(top, held[b, pl.ds(side * share, share), :])
 
+    diagonal = lax.broadcasted_iota(jnp.int32, (rows, rows), 0) == lax.broadcasted_iota(
+        jnp.int32, (rows, rows), 1
+    )
+
+    def as_row(col):
+        return jnp.sum(jnp.where(diagonal, col, 0.0), axis=0, keepdims=True)
+
+    def as_col(row):
+        return jnp.sum(jnp.where(diagonal, row, 0.0), axis=1, keepdims=True)
+
+    def swap_piece(src, dst, k, at):
+        part = pl.ds(k * piece, piece)
+        return send(src.at[:, part], dst.at[:, part], state_send.at[at + k], state_recv.at[at + k], across)
+
+    doc_pieces = [swap_piece(doc_ref, doc_came, k, 0) for k in range(pieces)]
+    query_pieces = [swap_piece(query_ref, query_came, k, pieces) for k in range(pieces)]
+    for copy in doc_pieces:
+        copy.start()
+
+    def left_of(which):
+        return left_ref[:, pl.ds(pl.multiple_of(which * depth, depth), depth)]
+
+    def project_mine(states, raw):
+        @pl.loop(0, tiles)
+        def _(n):
+            cols = pl.ds(pl.multiple_of(n * tile, tile), tile)
+            raw[:, cols] = dot_plain(states[...], weight[0, :, cols])
+
+    def project_piece(states, raw, k):
+        part = pl.ds(k * piece, piece)
+
+        @pl.loop(0, tiles)
+        def _(n):
+            cols = pl.ds(pl.multiple_of(n * tile, tile), tile)
+            raw[:, cols] += dot_plain(states[:, part], weight[1, part, cols])
+
+    def squares(raw):
+        def add(n, total):
+            block = raw[:, pl.ds(pl.multiple_of(n * 128, 128), 128)]
+            return total + block * block
+
+        total = lax.fori_loop(0, depth // 128, add, jnp.zeros((rows, 128), f32))
+        return jnp.sum(total, axis=1, keepdims=True)
+
+    def stat_copy(i):
+        return send(stat_out.at[i], stat_in.at[i], misc_send.at[i], misc_recv.at[i], across)
+
+    def normalize(raw, scale, store):
+        @pl.loop(0, tiles)
+        def _(n):
+            cols = pl.ds(pl.multiple_of(n * tile, tile), tile)
+            store(cols, (raw[:, cols] * scale).astype(bf16))
+
+    def store_doc(cols, value):
+        held[0, :, cols] = value
+
+    def store_query(cols, value):
+        top_ref[pl.ds(0, rows), cols] = value
+
+    loads[0].wait()
+    project_mine(doc_ref, doc_raw)
+    project_mine(query_ref, query_raw)
+    left_out[pl.ds(0, rows), :] = dot_rows(query_ref[...], left_of(side))
+    left_out[pl.ds(rows, rows), :] = dot_rows(doc_ref[...], left_of(side))
+    loads[1].wait()
+    for k in range(pieces):
+        doc_pieces[k].wait_recv()
+        project_piece(doc_came, doc_raw, k)
+    doc_sq = as_row(squares(doc_raw))
+    stat_out[0] = jnp.broadcast_to(doc_sq, (8, rows))
+    stat_copy(0).start()
+    for copy in query_pieces:
+        copy.start()
+    left_out[pl.ds(rows, rows), :] += dot_rows(doc_came[...], left_of(1 - side))
+    stat_copy(0).wait()
+    doc_scale = lax.rsqrt(doc_sq + stat_in[0, pl.ds(0, 1), :] + epsilon)
+    scale_out[...] = jnp.broadcast_to(doc_scale, (8, rows))
+    normalize(doc_raw, as_col(doc_scale), store_doc)
     to_right(1).start()
     to_left(1).start()
     to_sibling(0).start()
-    own = pltpu.make_async_copy(doc_ref, held.at[0], local_sem)
-    own.start()
-    qr_out[...] = dot_rows(top_ref[pl.ds(0, rows), :], top_ref[pl.ds(rows, width), :])
-    qrt_out[...] = dot_rows(top_ref[pl.ds(rows, width), :], top_ref[pl.ds(0, rows), :])
-    qr_swap = send(qr_out, qr_in, misc_send.at[0], misc_recv.at[0], across)
-    qrt_swap = send(qrt_out, qrt_in, misc_send.at[1], misc_recv.at[1], across)
-    qr_swap.start()
-    qrt_swap.start()
-    own.wait()
-    score(0)
-    to_sibling(0).wait_recv()
-    score(1)
+    top_ref[pl.ds(rows, width), :] = right_ref[...]
+    for k in range(pieces):
+        query_pieces[k].wait_recv()
+        project_piece(query_came, query_raw, k)
+    query_sq = squares(query_raw)
+    stat_out[1] = jnp.broadcast_to(as_row(query_sq), (8, rows))
+    stat_copy(1).start()
+    left_out[pl.ds(0, rows), :] += dot_rows(query_came[...], left_of(1 - side))
+    stat_copy(1).wait()
+    query_scale = lax.rsqrt(query_sq + as_col(stat_in[1, pl.ds(0, 1), :]) + epsilon)
+    normalize(query_raw, query_scale, store_query)
+    qr_swap = send(qr_out, qr_in, misc_send.at[3], misc_recv.at[3], across)
+    qrt_swap = send(qrt_out, qrt_in, misc_send.at[4], misc_recv.at[4], across)
     for s in range(1, half):
         to_right(s).wait_recv()
         to_right(s + 1).start()
@@ -218,6 +315,17 @@
         to_left(s).wait_recv()
         to_left(s + 1).start()
         to_sibling(s).start()
+        if s == 1:
+            qr_out[...] = dot_rows(top_ref[pl.ds(0, rows), :], top_ref[pl.ds(rows, width), :])
+            qrt_out[...] = dot_rows(top_ref[pl.ds(rows, width), :], top_ref[pl.ds(0, rows), :])
+            qr_swap.start()
+            qrt_swap.start()
+            to_sibling(0).wait_recv()
+
+            @pl.loop(0, 2)
+            def _(k):
+                score(k)
+
         to_sibling(chips - s).wait_recv()
         to_sibling(s).wait_recv()
 
@@ -236,6 +344,8 @@
         to_left(s).wait_send()
     for r in range(chips):
         to_sibling(r).wait_send()
+    for copy in doc_pieces + query_pieces:
+        copy.wait_send()
 
     def add_up(b, top):
         swap(b).wait()
@@ -251,28 +361,17 @@
 
     sum_wide = lax.fori_loop(0, dp_count, add_exp, jnp.zeros((rows, share), f32))
     sum_mine = jnp.sum(sum_wide, axis=1, keepdims=True)
-    diagonal = lax.broadcasted_iota(jnp.int32, (rows, rows), 0) == lax.broadcasted_iota(
-        jnp.int32, (rows, rows), 1
-    )
-
-    def as_row(col):
-        return jnp.sum(jnp.where(diagonal, col, 0.0), axis=0, keepdims=True)
-
-    def as_col(row):
-        return jnp.sum(jnp.where(diagonal, row, 0.0), axis=1, keepdims=True)
-
-    stat_out[...] = jnp.concatenate(
+    stat_out[2] = jnp.concatenate(
         [jnp.broadcast_to(as_row(top_mine), (4, rows)), jnp.broadcast_to(as_row(sum_mine), (4, rows))],
         axis=0,
     )
-    stat_swap = send(stat_out, stat_in, misc_send.at[2], misc_recv.at[2], across)
-    stat_swap.start()
+    stat_copy(2).start()
     qr_swap.wait()
     qrt_swap.wait()
     query_right = qr_out[...] + qr_in[...]
     turned_hi, turned_lo = hi_lo((qrt_out[...] + qrt_in[...]) * inverse_temp)
-    stat_swap.wait()
-    stats = stat_in[...]
+    stat_copy(2).wait()
+    stats = stat_in[2]
     top_other = as_col(stats[0:1])
     sum_other = as_col(stats[4:5])
     row_top = jnp.maximum(top_mine, top_other)
@@ -315,7 +414,7 @@
     carry = lax.fori_loop(1, dp_count, step, carry)
     query_sum, inner_wide = gradients(0, carry)
     query_send[...] = query_sum - jnp.sum(inner_wide, axis=1, keepdims=True) * query_right
-    query_swap = send(query_send, query_in, misc_send.at[3], misc_recv.at[3], across)
+    query_swap = send(query_send, query_in, misc_send.at[5], misc_recv.at[5], across)
     query_swap.start()
 
     @pl.loop(1, dp_count)
@@ -327,33 +426,42 @@
 
     doc_sum = lax.fori_loop(1, dp_count, collect, sum_out[0])
     doc_out[side] = doc_sum
-    last_swap = send(doc_out.at[side], last_in, misc_send.at[4], misc_recv.at[4], across)
+    last_swap = send(doc_out.at[side], last_in, misc_send.at[6], misc_recv.at[6], across)
     last_swap.start()
     query_swap.wait()
-    query_out[...] = query_send[...] + query_in[...]
+    query_out[...] = (query_send[...] + query_in[...]) * query_scale
     last_swap.wait()
     doc_out[1 - side] = last_in[...]
 
 
-def ring_gradients(top, docs, positives, dp_count, rows, share, width):
+def ring_gradients(query_states, doc_states, proj_weight, left_turned, right_turned, positives, dp_count):
     chips = dp_count // 2
-    depth = docs.shape[1]
+    rows, depth = doc_states.shape
+    share = rows // 2
+    width = right_turned.shape[0]
     dma = pltpu.SemaphoreType.DMA
     sums = pltpu.VMEM((dp_count, width, share), f32)
     parts = pltpu.VMEM((dp_count, rows + width, share), f32)
     vmem = pl.BlockSpec(memory_space=pltpu.VMEM)
+    raw = pltpu.VMEM((rows, depth), f32)
+    states = pltpu.VMEM((rows, depth), bf16)
     return pl.pallas_call(
         functools.partial(ring_kernel, dp_count, rows, share, width),
         out_shape=(
             jax.ShapeDtypeStruct((rows, width), f32),
             jax.ShapeDtypeStruct((2, width, share), f32),
+            jax.ShapeDtypeStruct((8, rows), f32),
+            jax.ShapeDtypeStruct((2 * rows, left_turned.shape[0]), f32),
         ),
-        in_specs=[vmem] * 3,
-        out_specs=(vmem, vmem),
+        in_specs=[vmem, vmem, pl.BlockSpec(memory_space=pl.ANY), vmem, vmem, vmem],
+        out_specs=(vmem, vmem, vmem, vmem),
         scratch_shapes=[
+            pltpu.VMEM((2, depth, depth), bf16),
+            raw, raw, states, states,
+            pltpu.VMEM((rows + width, depth), bf16),
             pltpu.VMEM((dp_count, rows, depth), bf16),
             parts, parts, parts,
-            pltpu.VMEM((8, rows), f32), pltpu.VMEM((8, rows), f32),
+            pltpu.VMEM((3, 8, rows), f32), pltpu.VMEM((3, 8, rows), f32),
             pltpu.VMEM((rows, width), f32), pltpu.VMEM((rows, width), f32),
             pltpu.VMEM((width, rows), f32), pltpu.VMEM((width, rows), f32),
             sums, sums,
@@ -361,27 +469,26 @@
             pltpu.VMEM((width, share), f32),
             dma((chips,)), dma((chips,)), dma((chips,)), dma, dma((chips,)), dma((chips,)),
             dma((dp_count,)), dma((dp_count,)), dma((dp_count,)), dma((dp_count,)),
-            dma((5,)), dma((5,)), dma,
+            dma((7,)), dma((7,)), dma((2,)), dma((2 * pieces,)), dma((2 * pieces,)),
         ],
         compiler_params=pltpu.CompilerParams(
-            collective_id=0, has_side_effects=True, vmem_limit_bytes=44 * 2**20
+            collective_id=0, has_side_effects=True, vmem_limit_bytes=57 * 2**20
         ),
-    )(top, docs, positives)
+    )(query_states, doc_states, proj_weight, left_turned, right_turned, positives)
 
 
 def local_ring(query_states, doc_states, proj_weight, left_proj, right_proj, positives):
     rank = lax.axis_index("tensor")
     rows = query_states.shape[0]
-    share = rows // 2
     depth = proj_weight.shape[1]
-    unit, scale, left = projected(query_states, doc_states, proj_weight, left_proj)
+    left_share = left_proj.shape[1] // 2
     right_mine = lax.dynamic_slice_in_dim(right_proj, rank * depth, depth, 0)
-    top = jnp.concatenate([unit[:rows], right_mine.T], axis=0)
-    right_query, right_doc = ring_gradients(
-        top, unit[rows:], positives[:, None], lax.axis_size("dp"), rows, share, right_proj.shape[1]
-    )
-    right_query = right_query * scale[:rows, None]
-    right_doc = right_doc.transpose(0, 2, 1).reshape(rows, -1) * scale[rows:, None]
+    left_mine = lax.dynamic_slice_in_dim(left_proj, rank * left_share, left_share, 1)
+    right_query, right_doc, scale, left = ring_gradients(
+        query_states, doc_states, proj_weight, left_mine.T, right_mine.T, positives[:, None],
+        lax.axis_size("dp"),
+    )
+    right_doc = right_doc.transpose(0, 2, 1).reshape(rows, -1) * scale[0][:, None]
     return (outer_rows(left[:rows], right_query), outer_rows(left[rows:], right_doc))
 
 

time: 173 us -> 139 us (0.80)
  waiting for transfers between devices: 34.3 us -> 0 us
  Pallas kernels: 102 us -> 126 us
  matrix products: 13.6 us -> 0 us
  other arithmetic: 5.86 us -> 0.47 us
  blocking collectives: 4.92 us -> 0 us
  starting transfers between devices: 3 us -> 0 us
  local copies, waits for them, and re-layouts: 8.31 us -> 11 us
    ppermute x1 -> x0, waiting for transfers between devices: 34.3 us -> none  [gather_columns(): other = lax.ppermute(block, 'tensor', [(0, 1), (1, 0)])]
    pallas_call x1, Pallas kernels: 102 us -> 126 us  [ring_gradients(): pl.pallas_call(functools.partial(ring_kernel, dp_count, rows, share, widt...]
    dot_general x2 -> x0, matrix products: 13.6 us -> none  [the longest x1 12.6 us: projected(): raw = jnp.dot(full, proj_weight, preferred_element_type=f32)]
    psum x1 -> x0, blocking collectives: 4.92 us -> none  [projected(): scale = lax.rsqrt(lax.psum(jnp.sum(raw * raw, axis=1), 'tensor') + epsilon)]
    unnamed x19 -> x4, local copies, waits for them, and re-layouts: 7.56 us -> 3.39 us
    transpose x2 -> x3, local copies, waits for them, and re-layouts: 0.08 us -> 3.28 us  [the longest x2 2.39 us: local_ring(): right_query, right_doc, scale, left = ring_gradients(query_states, doc_st...]
    ppermute x1 -> x0, starting transfers between devices: 3 us -> none  [gather_columns(): other = lax.ppermute(block, 'tensor', [(0, 1), (1, 0)])]
    convert_element_type x1 -> x0, other arithmetic: 2.18 us -> none  [projected(): unit = (raw * scale[:, None]).astype(bf16)]
  transfers between devices with their start and end apart: 1 -> 0, of which waited for: 1 -> 0; matrix products, arithmetic and copies ran while one was open for 0% -> 0% of each run, Pallas kernels for 0% -> 0%
where the time goes in v3:
time: 139 us
  Pallas kernels  126 us (91%)
  local copies, waits for them, and re-layouts  11 us (8%)
    pallas_call x1, Pallas kernels, ring_gradients(): pl.pallas_call(functools.partial(ring_kernel, dp_count, rows, share, widt...  126 us
    unnamed x4, local copies, waits for them, and re-layouts  3.39 us

profile of v3, /device:TPU:0, one launch (start us, length us, event | category | flops | bytes accessed | tf_op | source)
XLA Modules:
  0.0 138.6 jit_solution(9773981139721902041)
XLA Ops:
  0.6 0.0 copy-start
  0.6 1.5 %copy.8.pos_ref = s32[192,1]{1,0:T(8,128)} copy(s32[192,1]{0,1:T(1,128)} %bitcast.15) | data formatting | bytes 1536 | tf_op jit(solution)/shard_map/broadcast_in_dim | solution.py:488
  2.1 0.0 copy-done
  2.1 0.7 dynamic-slice_bitcast_fusion.1.left_ref
  2.9 1.7 %dynamic-slice_bitcast_fusion.right_ref = bf16[64,2048]{1,0:T(8,128)(2,1)} fusion(bf16[4096,64]{0,1:T(8,128)(2,1)} %param.10, s32[]{:T(128)S(6)} %select_n.7), kind=kLoop, calls=%fused_computation.2 | loop fusion | bytes 524292 | tf_op jit(solution)/shard_map/transpose | solution.py:488
  4.5 126.4 %shard_map.77 = (f32[192,64]{1,0:T(8,128)}, f32[2,64,96]{2,1,0:T(8,128)}, f32[8,192]{1,0:T(8,128)}, f32[384,32]{1,0:T(8,128)}) custom-call(bf16[192,2048]{1,0:T(8,128)(2,1)} %query_ref.1, bf16[192,2048]{1,0:T(8,128)(2,1)} %doc_ref.1, bf16[4096,2048]{1,0:T(8,128)(2,1)} %weight_ref.1, bf16[32,4096]{1,0:T(8,128)(2,1)} %dynamic-slice_bitcast_fusion.1.left_ref, ...), custom_call_target="tpu_custom_call" | custom-call | tf_op jit(solution)/shard_map/pallas_call | solution.py:448
  131.0 1.0 fusion
  131.9 0.1 copy.11
  132.0 0.7 slice.11
  132.7 0.1 copy.9
  132.8 1.0 copy.10
  133.8 0.9 copy.12
  134.7 0.1 reshape.37
  134.8 0.2 broadcast_multiply_fusion
  135.0 1.7 %copy.14 = f32[192,2048]{1,0:T(8,128)} copy(f32[192,2048]{0,1:T(8,128)S(1)} %bitcast.11) | data formatting | bytes 3145728
  136.7 0.2 broadcast_multiply_fusion.1
  136.9 1.7 %copy.13 = f32[192,2048]{1,0:T(8,128)} copy(f32[192,2048]{0,1:T(8,128)S(1)} %bitcast.12) | data formatting | bytes 3145728
  (1 shorter events, 0.0 us)
Async XLA Ops:
  0.6 1.5 %copy-start = (bf16[4096,64]{0,1:T(8,128)(2,1)S(1)}, bf16[4096,64]{0,1:T(8,128)(2,1)}, u32[]{:S(2)}) copy-start(bf16[4096,64]{0,1:T(8,128)(2,1)} %param.9) | copy-start | bytes 1572868

commit v4 on v3

--- a/solution.py
+++ b/solution.py
@@ -119,6 +119,10 @@
     return lax.dot_general(a, b, (((1,), (0,)), ((), ())), preferred_element_type=f32)
 
 
+def dot_down(a, b):
+    return lax.dot_general(a, b, (((0,), (0,)), ((), ())), preferred_element_type=f32)
+
+
 def hi_lo(value):
     hi = value.astype(bf16)
     return hi, (value - hi.astype(f32)).astype(bf16)
@@ -133,7 +137,7 @@
     query_ref, doc_ref, weight_ref, left_ref, right_ref, pos_ref,
     query_out, doc_out, scale_out, left_out,
     weight, query_raw, doc_raw, query_came, doc_came, top_ref,
-    held, mine, out_buf, in_buf, stat_out, stat_in, qr_out, qr_in, qrt_out, qrt_in,
+    held, full, mine, in_buf, stat_out, stat_in, qr_out, qr_in, qrt_out, qrt_in,
     sum_out, sum_in, query_send, query_in, last_in,
     right_send, left_send, ring_recv, half_recv, sib_send, sib_recv, x_send, x_recv,
     all_send, all_recv, misc_send, misc_recv, local_sem, state_send, state_recv,
@@ -205,14 +209,17 @@
     def to_sibling(r):
         return send(slot(r), held.at[2 * r + 1], sib_send.at[r], sib_recv.at[r], sibling)
 
+    my_docs = pl.ds(pl.multiple_of(side * share, share), share)
+    other_docs = pl.ds(pl.multiple_of((1 - side) * share, share), share)
+
     def swap(b):
-        return send(out_buf.at[b], in_buf.at[b], x_send.at[b], x_recv.at[b], across)
-
-    def score(b):
-        top = top_ref[...]
-        out_buf[b] = dot_rows(top, held[b, pl.ds((1 - side) * share, share), :])
-        swap(b).start()
-        mine[b] = dot_rows(top, held[b, pl.ds(side * share, share), :])
+        return send(full.at[b, other_docs], in_buf.at[b], x_send.at[b], x_recv.at[b], across)
+
+    def score(r):
+        both = held[pl.ds(2 * r, 2)].reshape(2 * rows, depth)
+        full[pl.ds(2 * r, 2)] = dot_rows(both, top_ref[...]).reshape(2, rows, rows + width)
+        swap(2 * r).start()
+        swap(2 * r + 1).start()
 
     diagonal = lax.broadcasted_iota(jnp.int32, (rows, rows), 0) == lax.broadcasted_iota(
         jnp.int32, (rows, rows), 1
@@ -322,23 +329,20 @@
             qrt_swap.start()
             to_sibling(0).wait_recv()
 
-            @pl.loop(0, 2)
-            def _(k):
-                score(k)
+            score(0)
 
         to_sibling(chips - s).wait_recv()
         to_sibling(s).wait_recv()
 
-        @pl.loop(0, 4)
+        @pl.loop(0, 2)
         def _(k):
-            score(2 * (s + (k % 2) * (chips - 2 * s)) + k // 2)
+            score(s + k * (chips - 2 * s))
 
     to_right(half).wait_recv()
     to_left(half).wait_recv()
     to_sibling(half).start()
-    score(2 * half)
     to_sibling(half).wait_recv()
-    score(2 * half + 1)
+    score(half)
     for s in range(1, half + 1):
         to_right(s).wait_send()
         to_left(s).wait_send()
@@ -349,31 +353,30 @@
 
     def add_up(b, top):
         swap(b).wait()
-        total = mine[b] + in_buf[b]
+        total = full[b, my_docs, :] + in_buf[b]
         mine[b] = total
-        return jnp.maximum(top, total[:rows] * inverse_temp)
-
-    top_wide = lax.fori_loop(0, dp_count, add_up, jnp.full((rows, share), -jnp.inf, f32))
-    top_mine = jnp.max(top_wide, axis=1, keepdims=True)
+        return jnp.maximum(top, total[:, :rows] * inverse_temp)
+
+    top_wide = lax.fori_loop(0, dp_count, add_up, jnp.full((share, rows), -jnp.inf, f32))
+    top_mine = jnp.max(top_wide, axis=0, keepdims=True)
 
     def add_exp(b, total):
-        return total + jnp.exp(mine[b, pl.ds(0, rows), :] * inverse_temp - top_mine)
-
-    sum_wide = lax.fori_loop(0, dp_count, add_exp, jnp.zeros((rows, share), f32))
-    sum_mine = jnp.sum(sum_wide, axis=1, keepdims=True)
+        return total + jnp.exp(mine[b, :, pl.ds(0, rows)] * inverse_temp - top_mine)
+
+    sum_wide = lax.fori_loop(0, dp_count, add_exp, jnp.zeros((share, rows), f32))
+    sum_mine = jnp.sum(sum_wide, axis=0, keepdims=True)
     stat_out[2] = jnp.concatenate(
-        [jnp.broadcast_to(as_row(top_mine), (4, rows)), jnp.broadcast_to(as_row(sum_mine), (4, rows))],
-        axis=0,
+        [jnp.broadcast_to(top_mine, (4, rows)), jnp.broadcast_to(sum_mine, (4, rows))], axis=0
     )
     stat_copy(2).start()
     qr_swap.wait()
     qrt_swap.wait()
-    query_right = qr_out[...] + qr_in[...]
-    turned_hi, turned_lo = hi_lo((qrt_out[...] + qrt_in[...]) * inverse_temp)
+    query_turned = qrt_out[...] + qrt_in[...]
+    right_hi, right_lo = hi_lo((qr_out[...] + qr_in[...]) * inverse_temp)
     stat_copy(2).wait()
     stats = stat_in[2]
-    top_other = as_col(stats[0:1])
-    sum_other = as_col(stats[4:5])
+    top_other = stats[0:1]
+    sum_other = stats[4:5]
     row_top = jnp.maximum(top_mine, top_other)
     lse = row_top + jnp.log(
         sum_mine * jnp.exp(top_mine - row_top) + sum_other * jnp.exp(top_other - row_top)
@@ -388,23 +391,24 @@
 
     def gradients(b, carry):
         query_sum, inner_wide = carry
-        scores = mine[b, pl.ds(0, rows), :] * inverse_temp
-        doc_right = mine[b, pl.ds(rows, width), :]
-        ids = lax.broadcasted_iota(jnp.int32, (rows, share), 1) + (
+        scores = mine[b, :, pl.ds(0, rows)] * inverse_temp
+        doc_right = mine[b][:, rows:]
+        ids = lax.broadcasted_iota(jnp.int32, (share, rows), 0) + (
             dp_at(b // 2, b % 2) * rows + side * share
         )
         onehot = jnp.where(positives == ids, 1.0, 0.0)
         weights = (jnp.exp(scores - lse) - onehot).astype(bf16)
         weighted = weights.astype(f32) * scores
-        right_hi, right_lo = hi_lo(doc_right * inverse_temp)
-        query_sum = query_sum + dot_rows(weights, right_hi) + dot_rows(weights, right_lo)
-        sum_out[b] = (
-            dot_plain(turned_hi, weights) + dot_plain(turned_lo, weights)
-            - jnp.sum(weighted, axis=0, keepdims=True) * doc_right
+        doc_hi, doc_lo = hi_lo(doc_right * inverse_temp)
+        query_sum = query_sum + dot_down(doc_hi, weights) + dot_down(doc_lo, weights)
+        doc_sum = (
+            dot_plain(weights, right_hi) + dot_plain(weights, right_lo)
+            - jnp.sum(weighted, axis=1, keepdims=True) * doc_right
         )
+        sum_out[b] = jnp.concatenate([doc_sum[: share // 2], doc_sum[share // 2 :]], axis=1)
         return query_sum, inner_wide + weighted
 
-    carry = (jnp.zeros((rows, width), f32), jnp.zeros((rows, share), f32))
+    carry = (jnp.zeros((width, rows), f32), jnp.zeros((share, rows), f32))
 
     def step(b, carry):
         carry = gradients(b, carry)
@@ -413,7 +417,7 @@
 
     carry = lax.fori_loop(1, dp_count, step, carry)
     query_sum, inner_wide = gradients(0, carry)
-    query_send[...] = query_sum - jnp.sum(inner_wide, axis=1, keepdims=True) * query_right
+    query_send[...] = query_sum - jnp.sum(inner_wide, axis=0, keepdims=True) * query_turned
     query_swap = send(query_send, query_in, misc_send.at[5], misc_recv.at[5], across)
     query_swap.start()
 
@@ -429,7 +433,7 @@
     last_swap = send(doc_out.at[side], last_in, misc_send.at[6], misc_recv.at[6], across)
     last_swap.start()
     query_swap.wait()
-    query_out[...] = (query_send[...] + query_in[...]) * query_scale
+    query_out[...] = (query_send[...] + query_in[...]) * as_row(query_scale)
     last_swap.wait()
     doc_out[1 - side] = last_in[...]
 
@@ -440,16 +444,16 @@
     share = rows // 2
     width = right_turned.shape[0]
     dma = pltpu.SemaphoreType.DMA
-    sums = pltpu.VMEM((dp_count, width, share), f32)
-    parts = pltpu.VMEM((dp_count, rows + width, share), f32)
+    sums = pltpu.VMEM((dp_count, share // 2, 2 * width), f32)
+    parts = pltpu.VMEM((dp_count, share, rows + width), f32)
     vmem = pl.BlockSpec(memory_space=pltpu.VMEM)
     raw = pltpu.VMEM((rows, depth), f32)
     states = pltpu.VMEM((rows, depth), bf16)
     return pl.pallas_call(
         functools.partial(ring_kernel, dp_count, rows, share, width),
         out_shape=(
-            jax.ShapeDtypeStruct((rows, width), f32),
-            jax.ShapeDtypeStruct((2, width, share), f32),
+            jax.ShapeDtypeStruct((width, rows), f32),
+            jax.ShapeDtypeStruct((2, share // 2, 2 * width), f32),
             jax.ShapeDtypeStruct((8, rows), f32),
             jax.ShapeDtypeStruct((2 * rows, left_turned.shape[0]), f32),
         ),
@@ -460,13 +464,13 @@
             raw, raw, states, states,
             pltpu.VMEM((rows + width, depth), bf16),
             pltpu.VMEM((dp_count, rows, depth), bf16),
-            parts, parts, parts,
+            pltpu.VMEM((dp_count, rows, rows + width), f32), parts, parts,
             pltpu.VMEM((3, 8, rows), f32), pltpu.VMEM((3, 8, rows), f32),
             pltpu.VMEM((rows, width), f32), pltpu.VMEM((rows, width), f32),
             pltpu.VMEM((width, rows), f32), pltpu.VMEM((width, rows), f32),
             sums, sums,
-            pltpu.VMEM((rows, width), f32), pltpu.VMEM((rows, width), f32),
-            pltpu.VMEM((width, share), f32),
+            pltpu.VMEM((width, rows), f32), pltpu.VMEM((width, rows), f32),
+            pltpu.VMEM((share // 2, 2 * width), f32),
             dma((chips,)), dma((chips,)), dma((chips,)), dma, dma((chips,)), dma((chips,)),
             dma((dp_count,)), dma((dp_count,)), dma((dp_count,)), dma((dp_count,)),
             dma((7,)), dma((7,)), dma((2,)), dma((2 * pieces,)), dma((2 * pieces,)),
@@ -485,11 +489,11 @@
     right_mine = lax.dynamic_slice_in_dim(right_proj, rank * depth, depth, 0)
     left_mine = lax.dynamic_slice_in_dim(left_proj, rank * left_share, left_share, 1)
     right_query, right_doc, scale, left = ring_gradients(
-        query_states, doc_states, proj_weight, left_mine.T, right_mine.T, positives[:, None],
+        query_states, doc_states, proj_weight, left_mine.T, right_mine.T, positives[None, :],
         lax.axis_size("dp"),
     )
-    right_doc = right_doc.transpose(0, 2, 1).reshape(rows, -1) * scale[0][:, None]
-    return (outer_rows(left[:rows], right_query), outer_rows(left[rows:], right_doc))
+    right_doc = jnp.stack(jnp.split(right_doc, 2, axis=2), axis=1).reshape(rows, -1) * scale[0][:, None]
+    return (outer_rows(left[:rows], right_query.T), outer_rows(left[rows:], right_doc))
 
 
 def solution(mesh):

time: 139 us -> 132 us (0.950)
  Pallas kernels: 126 us -> 120 us
    pallas_call x1, Pallas kernels: 126 us -> 120 us  [ring_gradients(): pl.pallas_call(functools.partial(ring_kernel, dp_count, rows, share, widt...]
    broadcast_in_dim x1 -> x0, local copies, waits for them, and re-layouts: 1.49 us -> none  [local_ring(): positives[:, None]]
    unnamed x4 -> x6, local copies, waits for them, and re-layouts: 3.39 us -> 4.42 us
where the time goes in v4:
time: 132 us; the launch traced here: 131 us
  Pallas kernels  120 us (91%)
  local copies, waits for them, and re-layouts  9.65 us (7%)
    pallas_call x1, Pallas kernels, ring_gradients(): pl.pallas_call(functools.partial(ring_kernel, dp_count, rows, share, widt...  120 us
    unnamed x6, local copies, waits for them, and re-layouts  4.42 us

profile of v4, /device:TPU:0, one launch (start us, length us, event | category | flops | bytes accessed | tf_op | source)
XLA Modules:
  0.0 131.3 jit_solution(13732226000567701553)
XLA Ops:
  0.6 0.0 copy-start
  0.6 1.0 copy-done
  1.7 0.7 dynamic-slice_bitcast_fusion.1.left_ref
  2.4 1.7 %dynamic-slice_bitcast_fusion.right_ref = bf16[64,2048]{1,0:T(8,128)(2,1)} fusion(bf16[4096,64]{0,1:T(8,128)(2,1)} %param.10, s32[]{:T(128)S(6)} %select_n.7), kind=kLoop, calls=%fused_computation.2 | loop fusion | bytes 524292 | tf_op jit(solution)/shard_map/transpose | solution.py:492
  4.1 120.3 %shard_map.77 = (f32[64,192]{1,0:T(8,128)}, f32[2,48,128]{2,1,0:T(8,128)}, f32[8,192]{1,0:T(8,128)}, f32[384,32]{1,0:T(8,128)}) custom-call(bf16[192,2048]{1,0:T(8,128)(2,1)} %query_ref.1, bf16[192,2048]{1,0:T(8,128)(2,1)} %doc_ref.1, bf16[4096,2048]{1,0:T(8,128)(2,1)} %weight_ref.1, bf16[32,4096]{1,0:T(8,128)(2,1)} %dynamic-slice_bitcast_fusion.1.left_ref, ...), custom_call_target="tpu_custom_call" | custom-call | tf_op jit(solution)/shard_map/pallas_call | solution.py:452
  124.4 1.0 fusion
  125.4 0.1 copy.10
  125.4 0.7 slice.11
  126.2 0.1 copy.9
  126.2 1.0 slice_bitcast_fusion.1
  127.2 0.1 bitcast_multiply_fusion
  127.3 0.1 copy.12
  127.4 0.2 broadcast_multiply_fusion
  127.6 0.0 copy-start.1
  127.6 1.7 %copy.14 = f32[192,2048]{1,0:T(8,128)} copy(f32[192,2048]{0,1:T(8,128)S(1)} %bitcast.15) | data formatting | bytes 3145728
  129.3 0.0 copy-done.1
  129.3 0.2 broadcast_multiply_fusion.1
  129.6 1.7 %copy.13 = f32[192,2048]{1,0:T(8,128)} copy(f32[192,2048]{0,1:T(8,128)S(1)} %bitcast.16) | data formatting | bytes 3145728
  (2 shorter events, 0.0 us)
Async XLA Ops:
  0.6 1.0 copy-start
  127.6 1.7 %copy-start.1 = (f32[64,192]{1,0:T(8,128)S(1)}, f32[64,192]{1,0:T(8,128)}, u32[]{:S(2)}) copy-start(f32[64,192]{1,0:T(8,128)} %get-tuple-element.7) | copy-start | bytes 147460

commit v5 on v4

--- a/solution.py
+++ b/solution.py
@@ -280,6 +280,14 @@
     def store_query(cols, value):
         top_ref[pl.ds(0, rows), cols] = value
 
+    def pass_on(s):
+        to_right(s).wait_recv()
+        to_right(s + 1).start()
+        to_sibling(chips - s).start()
+        to_left(s).wait_recv()
+        to_left(s + 1).start()
+        to_sibling(s).start()
+
     loads[0].wait()
     project_mine(doc_ref, doc_raw)
     project_mine(query_ref, query_raw)
@@ -310,18 +318,15 @@
     stat_out[1] = jnp.broadcast_to(as_row(query_sq), (8, rows))
     stat_copy(1).start()
     left_out[pl.ds(0, rows), :] += dot_rows(query_came[...], left_of(1 - side))
+    pass_on(1)
     stat_copy(1).wait()
     query_scale = lax.rsqrt(query_sq + as_col(stat_in[1, pl.ds(0, 1), :]) + epsilon)
     normalize(query_raw, query_scale, store_query)
     qr_swap = send(qr_out, qr_in, misc_send.at[3], misc_recv.at[3], across)
     qrt_swap = send(qrt_out, qrt_in, misc_send.at[4], misc_recv.at[4], across)
     for s in range(1, half):
-        to_right(s).wait_recv()
-        to_right(s + 1).start()
-        to_sibling(chips - s).start()
-        to_left(s).wait_recv()
-        to_left(s + 1).start()
-        to_sibling(s).start()
+        if s > 1:
+            pass_on(s)
         if s == 1:
             qr_out[...] = dot_rows(top_ref[pl.ds(0, rows), :], top_ref[pl.ds(rows, width), :])
             qrt_out[...] = dot_rows(top_ref[pl.ds(rows, width), :], top_ref[pl.ds(0, rows), :])
@@ -338,6 +343,15 @@
         def _(k):
             score(s + k * (chips - 2 * s))
 
+    def add_up(b, top):
+        swap(b).wait()
+        total = full[b, my_docs, :] + in_buf[b]
+        mine[b] = total
+        return jnp.maximum(top, total[:, :rows] * inverse_temp)
+
+    top_wide = jnp.full((share, rows), -jnp.inf, f32)
+    top_wide = lax.fori_loop(0, 2 * half - 2, add_up, top_wide)
+    top_wide = lax.fori_loop(2 * half + 4, dp_count, add_up, top_wide)
     to_right(half).wait_recv()
     to_left(half).wait_recv()
     to_sibling(half).start()
@@ -351,13 +365,7 @@
     for copy in doc_pieces + query_pieces:
         copy.wait_send()
 
-    def add_up(b, top):
-        swap(b).wait()
-        total = full[b, my_docs, :] + in_buf[b]
-        mine[b] = total
-        return jnp.maximum(top, total[:, :rows] * inverse_temp)
-
-    top_wide = lax.fori_loop(0, dp_count, add_up, jnp.full((share, rows), -jnp.inf, f32))
+    top_wide = lax.fori_loop(2 * half - 2, 2 * half + 4, add_up, top_wide)
     top_mine = jnp.max(top_wide, axis=0, keepdims=True)
 
     def add_exp(b, total):

time: 132 us -> 130 us (0.985)
  Pallas kernels: 120 us -> 118 us
    pallas_call x1, Pallas kernels: 120 us -> 118 us  [ring_gradients(): pl.pallas_call(functools.partial(ring_kernel, dp_count, rows, share, widt...]
where the time goes in v5:
time: 130 us; the launch traced here: 129 us
  Pallas kernels  118 us (91%)
  local copies, waits for them, and re-layouts  9.65 us (7%)
    pallas_call x1, Pallas kernels, ring_gradients(): pl.pallas_call(functools.partial(ring_kernel, dp_count, rows, share, widt...  118 us
    unnamed x6, local copies, waits for them, and re-layouts  4.42 us

profile of v5, /device:TPU:0, one launch (start us, length us, event | category | flops | bytes accessed | tf_op | source)
XLA Modules:
  0.0 129.4 jit_solution(10340847727171627270)
XLA Ops:
  0.6 0.0 copy-start
  0.6 1.0 copy-done
  1.7 0.7 dynamic-slice_bitcast_fusion.1.left_ref
  2.4 1.7 %dynamic-slice_bitcast_fusion.right_ref = bf16[64,2048]{1,0:T(8,128)(2,1)} fusion(bf16[4096,64]{0,1:T(8,128)(2,1)} %param.10, s32[]{:T(128)S(6)} %select_n.7), kind=kLoop, calls=%fused_computation.2 | loop fusion | bytes 524292 | tf_op jit(solution)/shard_map/transpose | solution.py:500
  4.1 118.5 %shard_map.77 = (f32[64,192]{1,0:T(8,128)}, f32[2,48,128]{2,1,0:T(8,128)}, f32[8,192]{1,0:T(8,128)}, f32[384,32]{1,0:T(8,128)}) custom-call(bf16[192,2048]{1,0:T(8,128)(2,1)} %query_ref.1, bf16[192,2048]{1,0:T(8,128)(2,1)} %doc_ref.1, bf16[4096,2048]{1,0:T(8,128)(2,1)} %weight_ref.1, bf16[32,4096]{1,0:T(8,128)(2,1)} %dynamic-slice_bitcast_fusion.1.left_ref, ...), custom_call_target="tpu_custom_call" | custom-call | tf_op jit(solution)/shard_map/pallas_call | solution.py:460
  122.6 1.0 fusion
  123.5 0.1 copy.10
  123.6 0.7 slice.11
  124.3 0.1 copy.9
  124.4 1.0 slice_bitcast_fusion.1
  125.4 0.1 bitcast_multiply_fusion
  125.5 0.1 copy.12
  125.6 0.2 broadcast_multiply_fusion
  125.8 0.0 copy-start.1
  125.8 1.7 %copy.14 = f32[192,2048]{1,0:T(8,128)} copy(f32[192,2048]{0,1:T(8,128)S(1)} %bitcast.15) | data formatting | bytes 3145728
  127.5 0.0 copy-done.1
  127.5 0.2 broadcast_multiply_fusion.1
  127.7 1.7 %copy.13 = f32[192,2048]{1,0:T(8,128)} copy(f32[192,2048]{0,1:T(8,128)S(1)} %bitcast.16) | data formatting | bytes 3145728
  (2 shorter events, 0.0 us)
Async XLA Ops:
  0.6 1.0 copy-start
  125.8 1.7 %copy-start.1 = (f32[64,192]{1,0:T(8,128)S(1)}, f32[64,192]{1,0:T(8,128)}, u32[]{:S(2)}) copy-start(f32[64,192]{1,0:T(8,128)} %get-tuple-element.7) | copy-start | bytes 147460
